TPU v7x, 256 devices: a whole 4x4x8 slice. The times are simulated.
256 devices in a mesh: grp: 16 (over x, y_lo, core), wk: 16 (over z, y_hi).
Axes of the slice: x: 4, y: 4 (y_hi: 2, y_lo: 2; y = y_hi * 2 + y_lo), z: 8, core: 2. Of those that a mesh axis runs over, the one named last changes fastest.
Arguments:
- owned_layer: int32 [16], replicated, may hold values from 0 to 15, each once
- wide_side: bfloat16 [16, 32768, 1024], P(None, ('grp', 'wk')), may hold values from -24 to 24
- narrow_side: bfloat16 [16, 32768, 256], P(None, ('grp', 'wk')), may hold values from -6 to 6
- wide_basis: float32 [16, 1024, 1024], P('grp', 'wk'), may hold values from -0.1875 to 0.1875
- narrow_basis: float32 [16, 256, 256], P('grp'), may hold values from -0.375 to 0.375
- wide_values: float32 [16, 1024], P('grp', 'wk'), may hold values from 0.001 to 0.1
- narrow_values: float32 [16, 256], P('grp'), may hold values from 0.001 to 0.1
Outputs:
- natural_grad: float32 [16, 1024, 256], P(None, 'wk')
Inputs may be any that keep to these rules, and one draw needn't show every extreme that they name: `owned_layer`: every layer is owned by exactly one group.
All inputs are finite; a program needn't handle non-finite values.
Results may differ from a plain program's by a relative error of at most 0.0003.
Values may be sent and summed in bfloat16 or wider, within the bound.
No kernel may reach another device: no remote copies, remote signals or barrier semaphores. Data moves between devices by JAX's collectives and lax.ppermute only.
A program may use at most 128 MiB of HBM per device.

v0:
```python
import jax
import jax.numpy as jnp
from jax import lax
from jax.sharding import PartitionSpec as P

DAMPING = 0.001


def local(
    owned_layer, wide_side, narrow_side, wide_basis, narrow_basis, wide_values, narrow_values
):
    highest = lax.Precision.HIGHEST
    groups = lax.axis_size("grp")
    workers = lax.axis_size("wk")
    total_tokens = wide_side.shape[1] * groups * workers
    partial_value = jnp.einsum(
        "ltc,ltk->lck", wide_side, narrow_side, preferred_element_type=jnp.float32
    )
    row_sums = lax.psum_scatter(partial_value, "wk", scatter_dimension=1, tiled=True)
    owned_rows = lax.psum_scatter(row_sums[owned_layer], "grp", scatter_dimension=0, tiled=True)[0]
    gradient = owned_rows / total_tokens
    basis_rows = wide_basis[0]
    basis_small = narrow_basis[0]
    columns = basis_rows
    rotated = lax.psum_scatter(
        jnp.dot(columns.T, gradient, precision=highest), "wk", scatter_dimension=0, tiled=True
    )
    rotated = jnp.dot(rotated, basis_small, precision=highest)
    scaled = rotated / (wide_values[0][:, None] * narrow_values[0][None, :] + DAMPING)
    returned = jnp.dot(scaled, basis_small.T, precision=highest)
    columns = basis_rows
    precond = jnp.dot(
        columns, lax.all_gather(returned, "wk", axis=0, tiled=True), precision=highest
    )
    gathered = lax.all_gather(precond[None], "grp", axis=0, tiled=True)
    return jnp.zeros_like(gathered).at[owned_layer].set(gathered)


def solution(mesh):
    return jax.shard_map(
        local,
        mesh=mesh,
        in_specs=(
            P(),
            P(None, ("grp", "wk"), None),
            P(None, ("grp", "wk"), None),
            P("grp", "wk", None),
            P("grp", None, None),
            P("grp", "wk"),
            P("grp", None),
        ),
        out_specs=P(None, "wk", None),
        check_vma=False,
    )
```

profile of v0, /device:TPU:1, one launch (start us, length us, event | category | flops | bytes accessed | tf_op | source)
XLA Modules:
  0.0 706.8 jit_solution(7205509945788100762)
XLA Ops:
  6.5 1.2 copy-done
  7.8 10.3 %fusion.9 = f32[16,1024,256]{2,1,0:T(8,128)} fusion(bf16[16,128,1024]{2,1,0:T(8,128)(2,1)} %param.8, bf16[16,128,256]{2,1,0:T(8,128)(2,1)S(1)} %copy-done), kind=kOutput, calls=%fused_computation.16 | convolution fusion | flops 1073741824 | bytes 22020096 | tf_op jit(solution)/shard_map/ltc,ltk->lck/dot_general | solution.py:16
  18.1 0.0 reduce-scatter.6.cloned.1.call-update
  18.1 0.0 reduce-scatter.8.cloned.1.call-start
  18.2 0.5 copy-done.5
  18.7 292.6 %reduce-scatter.6.cloned.1.call-done = f32[16,64,256]{2,1,0:T(8,128)} async-done(((f32[16,1024,256]{2,1,0:T(8,128)}), f32[16,64,256]{2,1,0:T(8,128)}) %reduce-scatter.6.cloned.1.call-update) | async-done | bytes 1048592 | tf_op jit(solution)/shard_map/reduce_scatter | solution.py:19
  311.3 2.8 gather_fusion
  314.1 0.0 reduce-scatter.8.cloned.1.call-update
  314.1 0.0 reduce-scatter.10.cloned.1.call-start
  314.2 58.5 %reduce-scatter.8.cloned.1.call-done = f32[1,64,256]{2,1,0:T(8,128)} async-done(((f32[16,64,256]{2,1,0:T(8,128)}), f32[1,64,256]{2,1,0:T(8,128)}) %reduce-scatter.8.cloned.1.call-update) | async-done | bytes 65552 | tf_op jit(solution)/shard_map/reduce_scatter | solution.py:20
  372.6 1.9 convolution_bitcast_fusion
  374.5 1.3 copy.12
  375.8 0.0 reduce-scatter.10.cloned.1.call-update
  375.8 0.0 all-gather.4.cloned.1.call-start
  375.9 200.8 %reduce-scatter.10.cloned.1.call-done = f32[64,256]{1,0:T(8,128)} async-done(((f32[1024,256]{1,0:T(8,128)}), f32[64,256]{1,0:T(8,128)}) %reduce-scatter.10.cloned.1.call-update) | async-done | bytes 65552
  576.7 1.1 convolution_divide_fusion
  577.8 1.0 fusion
  578.8 0.0 all-gather.4.cloned.1.call-update
  578.8 0.0 all-gather.6.cloned.1.call-start
  578.9 78.6 %all-gather.4.cloned.1.call-done = f32[1024,256]{1,0:T(8,128)} async-done(((f32[64,256]{1,0:T(8,128)}), f32[1024,256]{1,0:T(8,128)}) %all-gather.4.cloned.1.call-update) | async-done | bytes 1048592 | tf_op jit(solution)/shard_map/all_gather | solution.py:33
  657.5 2.6 convolution_bitcast_fusion.1
  660.1 35.8 %all-gather.6.cloned.1.call-done = f32[1024,256]{1,0:T(8,128)} async-done(((f32[64,256]{1,0:T(8,128)}), f32[1024,256]{1,0:T(8,128)}) %all-gather.6.cloned.1.call-update) | async-done | bytes 1048592 | tf_op jit(solution)/shard_map/all_gather | solution.py:35
  695.8 1.1 broadcast_in_dim.10
  696.9 3.4 scatter_fusion
  (14 shorter events, 0.1 us)
Async XLA Ops:
  6.5 1.2 copy-start
  6.5 304.8 %reduce-scatter.6.cloned.1.call-start = ((), (), s32[]{:S(2)}) async-start(), calls=%async_computation.3 | async-start | bytes 17825792 | tf_op jit(solution)/shard_map/reduce_scatter | solution.py:19
  18.1 0.7 copy-start.5
  18.1 354.6 %copy-start.2 = (f32[1,64,1024]{2,1,0:T(8,128)S(1)}, f32[1,64,1024]{2,1,0:T(8,128)}, u32[]{:S(2)}) copy-start(f32[1,64,1024]{2,1,0:T(8,128)} %param.10) | copy-start | bytes 786436
  18.1 558.6 %copy-start.1 = (f32[1,256,256]{2,1,0:T(8,128)S(1)}, f32[1,256,256]{2,1,0:T(8,128)}, u32[]{:S(2)}) copy-start(f32[1,256,256]{2,1,0:T(8,128)} %param.11) | copy-start | bytes 786436
  18.1 558.6 %copy-start.3 = (f32[1,256]{1,0:T(1,128)S(1)}, f32[1,256]{1,0:T(1,128)}, u32[]{:S(2)}) copy-start(f32[1,256]{1,0:T(1,128)} %param.13) | copy-start | bytes 3076
  18.1 558.6 %copy-start.4 = (f32[1,64]{1,0:T(1,128)S(1)}, f32[1,64]{1,0:T(1,128)}, u32[]{:S(2)}) copy-start(f32[1,64]{1,0:T(1,128)} %param.12) | copy-start | bytes 772
  18.1 354.5 %reduce-scatter.8.cloned.1.call-start = ((), (), s32[]{:S(2)}) async-start(), calls=%async_computation.4 | async-start | bytes 1114112 | tf_op jit(solution)/shard_map/reduce_scatter | solution.py:20
  314.1 262.6 %reduce-scatter.10.cloned.1.call-start = ((), (), s32[]{:S(2)}) async-start(), calls=%async_computation.7 | async-start | bytes 1114112
  375.8 281.6 %all-gather.4.cloned.1.call-start = ((), (), s32[]{:S(2)}) async-start(), calls=%async_computation.5 | async-start | bytes 1114112 | tf_op jit(solution)/shard_map/all_gather | solution.py:33
  578.8 117.0 %all-gather.6.cloned.1.call-start = ((), (), s32[]{:S(2)}) async-start(), calls=%async_computation.6 | async-start | bytes 1114112 | tf_op jit(solution)/shard_map/all_gather | solution.py:35
Sparse Core Ops, SparseCore 0:
  18.2 293.0 reduce-scatter.5
  314.2 58.3 reduce-scatter.7
  376.9 199.7 reduce-scatter.9
  579.5 77.9 all-gather.3
  660.2 35.5 all-gather.5
where the time goes:
time: 707 us
  waiting for transfers between devices  666 us (94%)
  matrix products  16.9 us (2%)
  between operations  13.2 us (2%)
  local copies, waits for them, and re-layouts  10.3 us (1%)
    reduce_scatter x1, waiting for transfers between devices, local(): lax.psum_scatter(partial_value, 'wk', scatter_dimension=1, tiled=True)  293 us
    unnamed x6, waiting for transfers between devices  201 us
    all_gather x1, waiting for transfers between devices, local(): lax.all_gather(returned, 'wk', axis=0, tiled=True)  78.6 us
    reduce_scatter x1, waiting for transfers between devices, local(): lax.psum_scatter(row_sums[owned_layer], 'grp', scatter_dimension=0, tiled...  58.5 us
    all_gather x1, waiting for transfers between devices, local(): gathered = lax.all_gather(precond[None], 'grp', axis=0, tiled=True)  35.8 us
  transfers between devices with their start and end apart: 5, of which 5 were waited for; matrix products, arithmetic and copies ran while one was open for 0% of the time, Pallas kernels for 0%

commit v1 on v0

v1 whole, which is shorter than its diff:
```python
import jax
import jax.numpy as jnp
from jax import lax
from jax.experimental import pallas as pl
from jax.experimental.pallas import tpu as pltpu
from jax.sharding import Mesh, PartitionSpec as P

DAMPING = 0.001
GRP = ("x", "yl", "core")
WK = ("z", "yh")
HIGH = lax.Precision.HIGH


def pack_kernel(owned_ref, wide_ref, narrow_ref, out_ref):
    wide = wide_ref.shape[2]
    out_ref[:, :, :wide] = wide_ref[...]
    out_ref[:, :, wide:] = narrow_ref[...]


def pack_tokens(owned_layer, wide_side, narrow_side):
    layers, tokens, wide = wide_side.shape
    narrow = narrow_side.shape[2]
    return pl.pallas_call(
        pack_kernel,
        out_shape=jax.ShapeDtypeStruct((layers, tokens, wide + narrow), wide_side.dtype),
        grid_spec=pltpu.PrefetchScalarGridSpec(
            num_scalar_prefetch=1,
            grid=(layers,),
            in_specs=[
                pl.BlockSpec((1, tokens, wide), lambda i, owned: (owned[i], 0, 0)),
                pl.BlockSpec((1, tokens, narrow), lambda i, owned: (owned[i], 0, 0)),
            ],
            out_specs=pl.BlockSpec((1, tokens, wide + narrow), lambda i, owned: (i, 0, 0)),
        ),
    )(owned_layer, wide_side, narrow_side)


def local(
    owned_layer, wide_side, narrow_side, wide_basis, narrow_basis, wide_values, narrow_values
):
    groups = lax.axis_size(GRP)
    workers = lax.axis_size(WK)
    layers, tokens, wide = wide_side.shape
    narrow = narrow_side.shape[2]
    total_tokens = tokens * groups * workers
    rows = wide // workers
    cols = narrow // workers

    values_row = jnp.pad(wide_values, ((0, 7), (0, wide - rows)))
    held = jnp.concatenate([wide_basis[0], values_row], axis=0)
    held = lax.all_gather(held, "yh", axis=0, tiled=False)
    held = lax.all_gather(held, "z", axis=0, tiled=False)
    held = held.reshape(workers, rows + 8, wide)
    basis = held[:, :rows].reshape(wide, wide)
    wide_all = held[:, rows, :rows].reshape(wide)

    packed = pack_tokens(owned_layer, wide_side, narrow_side)
    packed = lax.all_to_all(packed, GRP, 0, 0, tiled=True)
    packed = packed.reshape(groups * tokens, wide + narrow)
    partial = lax.dot_general(
        packed[:, wide:], packed[:, :wide], (((0,), (0,)), ((), ())),
        preferred_element_type=jnp.float32,
    )
    small = narrow_basis[0]
    partial = lax.dot_general(small, partial, (((0,), (0,)), ((), ())), precision=HIGH)
    partial = lax.all_to_all(partial.reshape(workers, cols, wide), WK, 0, 0, tiled=True)
    gradient = jnp.sum(partial, axis=0) / total_tokens
    rotated = jnp.dot(gradient, basis, precision=HIGH)
    worker = lax.axis_index(WK)
    values_small = lax.dynamic_slice(narrow_values[0], (worker * cols,), (cols,))
    scaled = rotated / (values_small[:, None] * wide_all[None, :] + DAMPING)
    precond = lax.dot_general(scaled, basis, (((1,), (1,)), ((), ())), precision=HIGH)
    precond = precond.reshape(cols, workers, rows).transpose(1, 0, 2)
    precond = lax.all_to_all(precond, WK, 0, 0, tiled=True).reshape(narrow, rows)
    mine = lax.dot_general(precond, small, (((0,), (1,)), ((), ())), precision=HIGH)
    gathered = lax.all_gather(mine, GRP, axis=0, tiled=False)
    return jnp.zeros_like(gathered).at[owned_layer].set(gathered)


def solution(mesh):
    fine = Mesh(
        mesh.devices.reshape(4, 2, 2, 8, 2), ("x", "yl", "core", "z", "yh")
    )
    return jax.shard_map(
        local,
        mesh=fine,
        in_specs=(
            P(),
            P(None, GRP + WK, None),
            P(None, GRP + WK, None),
            P(GRP, WK, None),
            P(GRP, None, None),
            P(GRP, WK),
            P(GRP, None),
        ),
        out_specs=P(None, WK, None),
        check_vma=False,
    )
```

time: 707 us -> 204 us (0.29)
  waiting for transfers between devices: 666 us -> 55.3 us
  blocking collectives: 0 us -> 94.5 us
  Pallas kernels: 0 us -> 11.1 us
  starting transfers between devices: 0.17 us -> 10.7 us
  matrix products: 16.9 us -> 7.46 us
    reduce_scatter x2 -> x0, waiting for transfers between devices: 351 us -> none  [the longest x1 293 us: local(): lax.psum_scatter(partial_value, 'wk', scatter_dimension=1, tiled=True)]
    unnamed x6 -> x2, waiting for transfers between devices: 201 us -> 0.03 us
    all_gather x2, waiting for transfers between devices: 114 us -> 29.4 us  [the longest x1 29.4 us: local(): gathered = lax.all_gather(mine, GRP, axis=0, tiled=False)]
    all_to_all x0 -> x2, blocking collectives: none -> 84.4 us  [the longest x1 68 us: local(): packed = lax.all_to_all(packed, GRP, 0, 0, tiled=True)]
    all_to_all x0 -> x1, waiting for transfers between devices: none -> 25.8 us  [local(): lax.all_to_all(partial.reshape(workers, cols, wide), WK, 0, 0, tiled=True)]
    pallas_call x0 -> x1, Pallas kernels: none -> 11.1 us  [pack_tokens(): pl.pallas_call(pack_kernel, out_shape=jax.ShapeDtypeStruct((layers, token...]
    all_to_all x0 -> x1, starting transfers between devices: none -> 10.6 us  [local(): lax.all_to_all(partial.reshape(workers, cols, wide), WK, 0, 0, tiled=True)]
    all_gather x0 -> x1, blocking collectives: none -> 10.1 us  [local(): held = lax.all_gather(held, 'yh', axis=0, tiled=False)]
  transfers between devices with their start and end apart: 5 -> 3, of which waited for: 5 -> 2; matrix products, arithmetic and copies ran while one was open for 0% -> 1% of each run, Pallas kernels for 0% -> 5%
where the time goes in v1:
time: 204 us; the launch traced here: 203 us
  blocking collectives  94.5 us (46%)
  waiting for transfers between devices  55.3 us (27%)
  between operations  13.5 us (7%)
  Pallas kernels  11.1 us (5%)
  starting transfers between devices  10.7 us (5%)
  local copies, waits for them, and re-layouts  8.63 us (4%)
  matrix products  7.46 us (4%)
    all_to_all x1, blocking collectives, local(): packed = lax.all_to_all(packed, GRP, 0, 0, tiled=True)  68 us
    all_gather x1, waiting for transfers between devices, local(): gathered = lax.all_gather(mine, GRP, axis=0, tiled=False)  29.4 us
    all_to_all x1, waiting for transfers between devices, local(): lax.all_to_all(partial.reshape(workers, cols, wide), WK, 0, 0, tiled=True)  25.8 us
    all_to_all x1, blocking collectives, local(): lax.all_to_all(precond, WK, 0, 0, tiled=True).reshape(narrow, rows)  16.5 us
    pallas_call x1, Pallas kernels, pack_tokens(): pl.pallas_call(pack_kernel, out_shape=jax.ShapeDtypeStruct((layers, token...  11.1 us
    all_to_all x1, starting transfers between devices, local(): lax.all_to_all(partial.reshape(workers, cols, wide), WK, 0, 0, tiled=True)  10.6 us
    all_gather x1, blocking collectives, local(): held = lax.all_gather(held, 'yh', axis=0, tiled=False)  10.1 us
  transfers between devices with their start and end apart: 3, of which 2 were waited for; matrix products, arithmetic and copies ran while one was open for 1% of the time, Pallas kernels for 5%

profile of v1, /device:TPU:1, one launch (start us, length us, event | category | flops | bytes accessed | tf_op | source)
XLA Modules:
  0.0 203.0 jit_solution(14568716480455873730)
XLA Ops:
  6.5 1.0 select_maximum_fusion
  7.6 10.1 %all-gather = f32[144,1024]{1,0:T(8,128)} all-gather(f32[72,1024]{1,0:T(8,128)S(1)} %select_maximum_fusion), channel_id=2, replica_groups=mesh['x'=4,'yl'=2,'core'=2,'z'=8,'yh'=2] {'yh'}, dimensions={0}, use_global_device_ids=true | all-gather | bytes 884736 | tf_op jit(solution)/shard_map/all_gather | solution.py:51
  17.7 11.1 %shard_map.73 = bf16[16,128,1280]{2,1,0:T(8,128)(2,1)} custom-call(s32[16]{0:T(128)} %owned_ref.1, bf16[16,128,1024]{2,1,0:T(8,128)(2,1)} %wide_ref.1, bf16[16,128,256]{2,1,0:T(8,128)(2,1)} %narrow_ref.1), custom_call_target="tpu_custom_call" | custom-call | tf_op jit(solution)/shard_map/pallas_call | solution.py:23
  28.8 68.0 %all_to_all.15 = bf16[16,128,1280]{2,1,0:T(8,128)(2,1)S(1)} all-to-all(bf16[16,128,1280]{2,1,0:T(8,128)(2,1)} %shard_map.73), channel_id=1, replica_groups=mesh['x'=4,'yl'=2,'core'=2,'z'=8,'yh'=2] {'x','yl','core'}, dimensions={0} | all-to-all | bytes 10485760 | tf_op jit(solution)/shard_map/all_to_all | solution.py:58
  96.7 1.3 fusion
  98.0 1.6 fusion.6
  99.6 10.6 %all-to-all-start.1 = ((f32[16,16,1024]{2,1,0:T(8,128)}), f32[16,16,1024]{2,1,0:T(8,128)S(1)}, u32[]{:S(2)}, u32[]{:S(2)}) async-start(f32[16,16,1024]{2,1,0:T(8,128)} %bitcast.3), calls=%async_computation.1 | async-start | bytes 2097152 | tf_op jit(solution)/shard_map/all_to_all | solution.py:66
  110.3 0.1 dynamic-slice_bitcast_fusion
  110.4 25.8 %all-to-all-done.1 = f32[16,16,1024]{2,1,0:T(8,128)S(1)} async-done(((f32[16,16,1024]{2,1,0:T(8,128)}), f32[16,16,1024]{2,1,0:T(8,128)S(1)}, u32[]{:S(2)}, u32[]{:S(2)}) %all-to-all-start.1) | async-done | bytes 1048608 | tf_op jit(solution)/shard_map/all_to_all | solution.py:66
  136.3 0.9 slice_reduce_fusion
  137.2 0.1 mul.27
  137.3 2.3 %slice-done.2 = f32[16,64,1024]{2,1,0:T(8,128)S(1)} async-done(((f32[16,72,1024]{2,1,0:T(8,128)}), f32[16,64,1024]{2,1,0:T(8,128)S(1)}, s32[]{:S(2)}) %slice-start.2) | async-done | bytes 4194328 | tf_op jit(solution)/shard_map/slice | solution.py:54
  139.6 1.1 fusion.2
  140.7 0.1 slice-done.1
  140.8 2.5 %convolution_bitcast_fusion = f32[16,16,64]{2,1,0:T(8,128)S(1)} fusion(f32[16,1024,1]{1,0,2:T(8,128)S(1)} %fusion.2, f32[16,72,1024]{2,1,0:T(8,128)S(1)} %bitcast.25), kind=kOutput, calls=%fused_computation.3 | convolution fusion | flops 100663296 | bytes 4325376 | tf_op jit(solution)/shard_map/dot_general | solution.py:72
  143.4 0.1 reshape.48
  143.5 16.5 %all_to_all.16 = f32[16,1,1024]{2,1,0:T(1,128)S(1)} all-to-all(f32[16,1,1024]{2,1,0:T(1,128)S(1)} %reshape.48), channel_id=1, replica_groups=mesh['x'=4,'yl'=2,'core'=2,'z'=8,'yh'=2] {'z','yh'}, dimensions={0} | all-to-all | bytes 131072 | tf_op jit(solution)/shard_map/all_to_all | solution.py:74
  160.0 0.5 broadcast.20
  160.5 0.8 reduce.4
  161.3 0.1 reshape.49
  161.4 0.9 fusion.4
  162.3 29.4 %all-gather.8.cloned.1.call-done = f32[1024,256]{1,0:T(8,128)} async-done(((f32[64,256]{1,0:T(8,128)}), f32[1024,256]{1,0:T(8,128)}) %all-gather.8.cloned.1.call-update) | async-done | bytes 1048592 | tf_op jit(solution)/shard_map/all_gather | solution.py:76
  191.7 1.1 broadcast_in_dim.7
  192.8 3.4 %scatter_fusion = f32[16,64,256]{2,1,0:T(8,128)} fusion(f32[16,64,256]{2,1,0:T(8,128)} %broadcast_in_dim.7, s32[16]{0:T(128)S(1)} %compare_select_fusion, f32[16,64,256]{2,1,0:T(8,128)} %bitcast.29), kind=kCustom, calls=%fused_computation | custom fusion | bytes 3145792 | tf_op jit(solution)/shard_map/scatter | solution.py:77
  (18 shorter events, 0.2 us)
Async XLA Ops:
  6.5 91.5 %copy-start = (f32[1,256,256]{2,1,0:T(8,128)S(1)}, f32[1,256,256]{2,1,0:T(8,128)}, u32[]{:S(2)}) copy-start(f32[1,256,256]{2,1,0:T(8,128)} %param.11) | copy-start | bytes 786436
  6.5 129.8 %all-gather.6.cloned.1.call-start = ((), (), s32[]{:S(2)}) async-start(), calls=%async_computation.3 | async-start | bytes 5308416 | tf_op jit(solution)/shard_map/all_gather | solution.py:52
  96.7 13.6 %copy-start.2 = (f32[1,256]{1,0:T(1,128)S(1)}, f32[1,256]{1,0:T(1,128)}, u32[]{:S(2)}) copy-start(f32[1,256]{1,0:T(1,128)} %param.13) | copy-start | bytes 3076
  99.6 36.6 %all-to-all-start.1 = ((f32[16,16,1024]{2,1,0:T(8,128)}), f32[16,16,1024]{2,1,0:T(8,128)S(1)}, u32[]{:S(2)}, u32[]{:S(2)}) async-start(f32[16,16,1024]{2,1,0:T(8,128)} %bitcast.3), calls=%async_computation.1 | async-start | bytes 2097152 | tf_op jit(solution)/shard_map/all_to_all | solution.py:66
  110.3 81.5 %all-gather.8.cloned.1.call-start = ((), (), s32[]{:S(2)}) async-start(), calls=%async_computation.4 | async-start | bytes 1114112 | tf_op jit(solution)/shard_map/all_gather | solution.py:76
  137.2 3.5 %slice-start = ((s8[4718592]{0:T(1024)(128)(4,1)}), s8[524288]{0:T(1024)(128)(4,1)S(1)}, s32[]{:S(2)}) async-start(s8[4718592]{0:T(1024)(128)(4,1)} %bitcast.24), calls=%async_computation.5 | async-start | bytes 1048576
  137.3 2.3 %slice-start.2 = ((f32[16,72,1024]{2,1,0:T(8,128)}), f32[16,64,1024]{2,1,0:T(8,128)S(1)}, s32[]{:S(2)}) async-start(f32[16,72,1024]{2,1,0:T(8,128)} %all-gather.6.cloned.1.call-done), calls=%async_computation.7 | async-start | bytes 8388608 | tf_op jit(solution)/shard_map/slice | solution.py:54
  137.3 3.6 %slice-start.1 = ((s8[4718592]{0:T(1024)(128)(4,1)}), s8[4194304]{0:T(1024)(128)(4,1)S(1)}, s32[]{:S(2)}) async-start(s8[4718592]{0:T(1024)(128)(4,1)} %bitcast.24), calls=%async_computation.6 | async-start | bytes 8388608
  139.6 22.8 %copy-start.1 = (s32[16]{0:T(128)S(1)}, s32[16]{0:T(128)}, u32[]{:S(2)}) copy-start(s32[16]{0:T(128)} %owned_ref.1) | copy-start | bytes 196
Sparse Core Ops, SparseCore 0:
  17.8 64.4 all-gather.5
  162.4 29.2 all-gather.7

commit v2 on v1

--- a/solution.py
+++ b/solution.py
@@ -9,12 +9,29 @@
 GRP = ("x", "yl", "core")
 WK = ("z", "yh")
 HIGH = lax.Precision.HIGH
+PACK_SPACE = pltpu.VMEM
 
 
-def pack_kernel(owned_ref, wide_ref, narrow_ref, out_ref):
-    wide = wide_ref.shape[2]
-    out_ref[:, :, :wide] = wide_ref[...]
-    out_ref[:, :, wide:] = narrow_ref[...]
+def pack_kernel(owned_ref, wide_ref, narrow_ref, out_ref, sems):
+    layers, _, wide = wide_ref.shape
+    narrow = narrow_ref.shape[2]
+    copies = []
+    for group in range(layers):
+        layer = owned_ref[group]
+        copies.append(
+            pltpu.make_async_copy(
+                wide_ref.at[layer], out_ref.at[group, :, pl.ds(0, wide)], sems.at[group, 0]
+            )
+        )
+        copies.append(
+            pltpu.make_async_copy(
+                narrow_ref.at[layer], out_ref.at[group, :, pl.ds(wide, narrow)], sems.at[group, 1]
+            )
+        )
+    for copy in copies:
+        copy.start()
+    for copy in copies:
+        copy.wait()
 
 
 def pack_tokens(owned_layer, wide_side, narrow_side):
@@ -23,16 +40,51 @@
     return pl.pallas_call(
         pack_kernel,
         out_shape=jax.ShapeDtypeStruct((layers, tokens, wide + narrow), wide_side.dtype),
-        grid_spec=pltpu.PrefetchScalarGridSpec(
-            num_scalar_prefetch=1,
-            grid=(layers,),
-            in_specs=[
-                pl.BlockSpec((1, tokens, wide), lambda i, owned: (owned[i], 0, 0)),
-                pl.BlockSpec((1, tokens, narrow), lambda i, owned: (owned[i], 0, 0)),
-            ],
-            out_specs=pl.BlockSpec((1, tokens, wide + narrow), lambda i, owned: (i, 0, 0)),
-        ),
+        in_specs=[
+            pl.BlockSpec(memory_space=pltpu.SMEM),
+            pl.BlockSpec(memory_space=pl.ANY),
+            pl.BlockSpec(memory_space=pl.ANY),
+        ],
+        out_specs=pl.BlockSpec(memory_space=PACK_SPACE),
+        scratch_shapes=[pltpu.SemaphoreType.DMA((layers, 2))],
     )(owned_layer, wide_side, narrow_side)
+
+
+def place_kernel(owned_ref, core_ref, mine_ref, other_ref, out_ref, sems):
+    core = core_ref[0]
+    chips = mine_ref.shape[0]
+    copies = []
+    for chip in range(chips):
+        copies.append(
+            pltpu.make_async_copy(
+                mine_ref.at[chip], out_ref.at[owned_ref[2 * chip + core]], sems.at[chip, 0]
+            )
+        )
+        copies.append(
+            pltpu.make_async_copy(
+                other_ref.at[chip], out_ref.at[owned_ref[2 * chip + 1 - core]], sems.at[chip, 1]
+            )
+        )
+    for copy in copies:
+        copy.start()
+    for copy in copies:
+        copy.wait()
+
+
+def place(owned_layer, core, mine, other):
+    chips, rows, narrow = mine.shape
+    return pl.pallas_call(
+        place_kernel,
+        out_shape=jax.ShapeDtypeStruct((2 * chips, rows, narrow), mine.dtype),
+        in_specs=[
+            pl.BlockSpec(memory_space=pltpu.SMEM),
+            pl.BlockSpec(memory_space=pltpu.SMEM),
+            pl.BlockSpec(memory_space=pltpu.VMEM),
+            pl.BlockSpec(memory_space=pltpu.VMEM),
+        ],
+        out_specs=pl.BlockSpec(memory_space=pl.ANY),
+        scratch_shapes=[pltpu.SemaphoreType.DMA((chips, 2))],
+    )(owned_layer, core, mine, other)
 
 
 def local(
@@ -46,15 +98,20 @@
     rows = wide // workers
     cols = narrow // workers
 
+    packed = pack_tokens(owned_layer, wide_side, narrow_side)
     values_row = jnp.pad(wide_values, ((0, 7), (0, wide - rows)))
     held = jnp.concatenate([wide_basis[0], values_row], axis=0)
-    held = lax.all_gather(held, "yh", axis=0, tiled=False)
+    swapped = lax.ppermute(held, "yh", [(0, 1), (1, 0)])
+    low = lax.axis_index("yh") == 0
+    held = jnp.stack([jnp.where(low, held, swapped), jnp.where(low, swapped, held)])
+    worker = lax.axis_index(WK)
+    values_small = lax.dynamic_slice(narrow_values[0], (worker * cols,), (cols,))
+    held, packed, values_small = lax.optimization_barrier((held, packed, values_small))
     held = lax.all_gather(held, "z", axis=0, tiled=False)
     held = held.reshape(workers, rows + 8, wide)
     basis = held[:, :rows].reshape(wide, wide)
     wide_all = held[:, rows, :rows].reshape(wide)
 
-    packed = pack_tokens(owned_layer, wide_side, narrow_side)
     packed = lax.all_to_all(packed, GRP, 0, 0, tiled=True)
     packed = packed.reshape(groups * tokens, wide + narrow)
     partial = lax.dot_general(
@@ -66,15 +123,15 @@
     partial = lax.all_to_all(partial.reshape(workers, cols, wide), WK, 0, 0, tiled=True)
     gradient = jnp.sum(partial, axis=0) / total_tokens
     rotated = jnp.dot(gradient, basis, precision=HIGH)
-    worker = lax.axis_index(WK)
-    values_small = lax.dynamic_slice(narrow_values[0], (worker * cols,), (cols,))
     scaled = rotated / (values_small[:, None] * wide_all[None, :] + DAMPING)
     precond = lax.dot_general(scaled, basis, (((1,), (1,)), ((), ())), precision=HIGH)
     precond = precond.reshape(cols, workers, rows).transpose(1, 0, 2)
     precond = lax.all_to_all(precond, WK, 0, 0, tiled=True).reshape(narrow, rows)
     mine = lax.dot_general(precond, small, (((0,), (1,)), ((), ())), precision=HIGH)
-    gathered = lax.all_gather(mine, GRP, axis=0, tiled=False)
-    return jnp.zeros_like(gathered).at[owned_layer].set(gathered)
+    spread = jnp.broadcast_to(mine[None], (groups // 2,) + mine.shape)
+    spread = lax.all_to_all(spread, ("x", "yl"), 0, 0, tiled=True)
+    other = lax.ppermute(spread, "core", [(0, 1), (1, 0)])
+    return place(owned_layer, lax.axis_index("core").reshape(1), spread, other)
 
 
 def solution(mesh):

time: 204 us -> 175 us (0.86)
  waiting for transfers between devices: 55.3 us -> 1.58 us
  blocking collectives: 94.5 us -> 130 us
  local copies, waits for them, and re-layouts: 8.63 us -> 5.01 us
  starting transfers between devices: 10.7 us -> 7.45 us
  Pallas kernels: 11.1 us -> 8.13 us
    all_to_all x0 -> x2, blocking collectives: none -> 49.5 us  [the longest x1 38.4 us: local(): lax.all_to_all(partial.reshape(workers, cols, wide), WK, 0, 0, tiled=True)]
    all_gather x1 -> x0, waiting for transfers between devices: 29.4 us -> none  [local(): gathered = lax.all_gather(mine, GRP, axis=0, tiled=False)]
    all_to_all x1 -> x0, waiting for transfers between devices: 25.8 us -> none  [local(): lax.all_to_all(partial.reshape(workers, cols, wide), WK, 0, 0, tiled=True)]
    all_to_all x1 -> x0, starting transfers between devices: 10.6 us -> none  [local(): lax.all_to_all(partial.reshape(workers, cols, wide), WK, 0, 0, tiled=True)]
    all_gather x1 -> x0, blocking collectives: 10.1 us -> none  [local(): held = lax.all_gather(held, 'yh', axis=0, tiled=False)]
    ppermute x0 -> x2, starting transfers between devices: none -> 7.44 us  [the longest x1 3.83 us: local(): swapped = lax.ppermute(held, 'yh', [(0, 1), (1, 0)])]
    pallas_call x1, Pallas kernels: 11.1 us -> 5.83 us  [pack_tokens(): pl.pallas_call(pack_kernel, out_shape=jax.ShapeDtypeStruct((layers, token...]
    scatter x1 -> x0, local copies, waits for them, and re-layouts: 3.37 us -> none  [local(): return jnp.zeros_like(gathered).at[owned_layer].set(gathered)]
  transfers between devices with their start and end apart: 3 -> 3, of which waited for: 2 -> 1; matrix products, arithmetic and copies ran while one was open for 1% -> 1% of each run, Pallas kernels for 5% -> 3%
where the time goes in v2:
time: 175 us
  blocking collectives  130 us (74%)
  between operations  13.5 us (8%)
  Pallas kernels  8.13 us (5%)
  starting transfers between devices  7.45 us (4%)
  matrix products  5.84 us (3%)
  local copies, waits for them, and re-layouts  5.01 us (3%)
  other arithmetic  2.81 us (2%)
    all_to_all x1, blocking collectives, local(): packed = lax.all_to_all(packed, GRP, 0, 0, tiled=True)  67.6 us
    all_to_all x1, blocking collectives, local(): lax.all_to_all(partial.reshape(workers, cols, wide), WK, 0, 0, tiled=True)  38.4 us
    all_to_all x1, blocking collectives, local(): lax.all_to_all(precond, WK, 0, 0, tiled=True).reshape(narrow, rows)  13.4 us
    all_to_all x1, blocking collectives, local(): spread = lax.all_to_all(spread, ('x', 'yl'), 0, 0, tiled=True)  11.1 us
    pallas_call x1, Pallas kernels, pack_tokens(): pl.pallas_call(pack_kernel, out_shape=jax.ShapeDtypeStruct((layers, token...  5.83 us
    ppermute x1, starting transfers between devices, local(): swapped = lax.ppermute(held, 'yh', [(0, 1), (1, 0)])  3.83 us
    ppermute x1, starting transfers between devices, local(): other = lax.ppermute(spread, 'core', [(0, 1), (1, 0)])  3.61 us
  transfers between devices with their start and end apart: 3, of which 1 were waited for; matrix products, arithmetic and copies ran while one was open for 1% of the time, Pallas kernels for 3%

profile of v2, /device:TPU:1, one launch (start us, length us, event | category | flops | bytes accessed | tf_op | source)
XLA Modules:
  0.0 174.8 jit_solution(16489699484086201660)
XLA Ops:
  6.5 1.0 select_maximum_fusion
  7.6 3.8 %collective-permute-start = (f32[72,1024]{1,0:T(8,128)S(1)}, f32[72,1024]{1,0:T(8,128)S(1)}, u32[]{:S(2)}, u32[]{:S(2)}) collective-permute-start(f32[72,1024]{1,0:T(8,128)S(1)} %select_maximum_fusion), channel_id=1, source_target_pairs={{0,1},{1,0},{2,3},{3,2},{4,5},{5,4},{6,7},{7,6},{8,9},{9,8},{10,11... | collective-permute-start | bytes 884744 | tf_op jit(solution)/shard_map/ppermute | solution.py:104
  11.4 5.8 %shard_map.73 = bf16[16,128,1280]{2,1,0:T(8,128)(2,1)} custom-call(s32[16]{0:T(128)} %owned_ref.3, bf16[16,128,1024]{2,1,0:T(8,128)(2,1)} %wide_ref.1, bf16[16,128,256]{2,1,0:T(8,128)(2,1)} %narrow_ref.1), custom_call_target="tpu_custom_call" | custom-call | tf_op jit(solution)/shard_map/pallas_call | solution.py:40
  17.4 0.9 pad_maximum_fusion
  18.3 67.6 %all_to_all.20 = bf16[16,128,1280]{2,1,0:T(8,128)(2,1)S(1)} all-to-all(bf16[16,128,1280]{2,1,0:T(8,128)(2,1)} %shard_map.73), channel_id=1, replica_groups=mesh['x'=4,'yl'=2,'core'=2,'z'=8,'yh'=2] {'x','yl','core'}, dimensions={0} | all-to-all | bytes 10485760 | tf_op jit(solution)/shard_map/all_to_all | solution.py:115
  85.9 1.3 fusion
  87.2 0.6 fusion.6
  87.8 38.4 %all_to_all.21 = f32[16,16,1024]{2,1,0:T(8,128)S(1)} all-to-all(f32[16,16,1024]{2,1,0:T(8,128)S(1)} %bitcast.31), channel_id=1, replica_groups=mesh['x'=4,'yl'=2,'core'=2,'z'=8,'yh'=2] {'z','yh'}, dimensions={0} | all-to-all | bytes 2097152 | tf_op jit(solution)/shard_map/all_to_all | solution.py:123
  126.3 0.9 slice_reduce_fusion
  127.3 2.3 %slice-done.2 = f32[16,64,1024]{2,1,0:T(8,128)S(1)} async-done(((f32[16,72,1024]{2,1,0:T(8,128)}), f32[16,64,1024]{2,1,0:T(8,128)S(1)}, s32[]{:S(2)}) %slice-start.2) | async-done | bytes 4194328 | tf_op jit(solution)/shard_map/slice | solution.py:112
  129.5 1.1 fusion.2
  130.7 0.1 slice-done.1
  130.8 2.5 %convolution_bitcast_fusion = f32[16,16,64]{2,1,0:T(8,128)S(1)} fusion(f32[16,1024,1]{1,0,2:T(8,128)S(1)} %fusion.2, f32[16,72,1024]{2,1,0:T(8,128)S(1)} %bitcast.28), kind=kOutput, calls=%fused_computation.2 | convolution fusion | flops 100663296 | bytes 4325376 | tf_op jit(solution)/shard_map/dot_general | solution.py:127
  133.4 0.1 reshape.41
  133.5 13.4 %all_to_all.22 = f32[16,1,1024]{2,1,0:T(1,128)S(1)} all-to-all(f32[16,1,1024]{2,1,0:T(1,128)S(1)} %reshape.41), channel_id=1, replica_groups=mesh['x'=4,'yl'=2,'core'=2,'z'=8,'yh'=2] {'z','yh'}, dimensions={0} | all-to-all | bytes 131072 | tf_op jit(solution)/shard_map/all_to_all | solution.py:129
  146.9 0.5 broadcast.20
  147.4 0.8 reduce.4
  148.2 0.1 reshape.42
  148.3 0.3 fusion.4
  148.6 11.1 %all_to_all.23.mine_ref = f32[8,64,256]{2,1,0:T(8,128)S(1)} all-to-all(f32[8,64,256]{2,1,0:T(8,128)S(1)} %broadcast_in_dim.2), channel_id=1, replica_groups=mesh['x'=4,'yl'=2,'core'=2,'z'=8,'yh'=2] {'x','yl'}, dimensions={0} | all-to-all | bytes 1048576 | tf_op jit(solution)/shard_map/all_to_all | solution.py:132
  159.7 3.6 %collective-permute-start.1 = (f32[8,64,256]{2,1,0:T(8,128)S(1)}, f32[8,64,256]{2,1,0:T(8,128)S(1)}, u32[]{:S(2)}, u32[]{:S(2)}) collective-permute-start(f32[8,64,256]{2,1,0:T(8,128)S(1)} %all_to_all.23.mine_ref), channel_id=1, source_target_pairs={{0,16},{16,0},{1,17},{17,1},{2,18},{18,2},{3,19},{19,3},{4,20},{20... | collective-permute-start | bytes 1572872 | tf_op jit(solution)/shard_map/ppermute | solution.py:133
  163.3 1.5 collective-permute-done.1.other_ref
  164.9 0.8 copy-done.3
  165.6 2.3 %shard_map.74 = f32[16,64,256]{2,1,0:T(8,128)} custom-call(s32[16]{0:T(128)} %owned_ref.3, s32[1]{0:T(128)} %bitcast.core_ref, f32[8,64,256]{2,1,0:T(8,128)} %copy-done.1, f32[8,64,256]{2,1,0:T(8,128)} %copy-done.3), custom_call_target="tpu_custom_call" | custom-call | tf_op jit(solution)/shard_map/pallas_call | solution.py:76
  (25 shorter events, 0.4 us)
Async XLA Ops:
  6.5 80.6 %copy-start = (f32[1,256,256]{2,1,0:T(8,128)S(1)}, f32[1,256,256]{2,1,0:T(8,128)}, u32[]{:S(2)}) copy-start(f32[1,256,256]{2,1,0:T(8,128)} %param.11) | copy-start | bytes 786436
  6.5 119.8 %all-gather.3.cloned.1.call-start = ((), (), s32[]{:S(2)}) async-start(), calls=%async_computation.4 | async-start | bytes 5308416 | tf_op jit(solution)/shard_map/all_gather | solution.py:110
  7.6 9.8 %collective-permute-start = (f32[72,1024]{1,0:T(8,128)S(1)}, f32[72,1024]{1,0:T(8,128)S(1)}, u32[]{:S(2)}, u32[]{:S(2)}) collective-permute-start(f32[72,1024]{1,0:T(8,128)S(1)} %select_maximum_fusion), channel_id=1, source_target_pairs={{0,1},{1,0},{2,3},{3,2},{4,5},{5,4},{6,7},{7,6},{8,9},{9,8},{10,11... | collective-permute-start | bytes 884744 | tf_op jit(solution)/shard_map/ppermute | solution.py:104
  11.4 5.8 %copy-start.5 = (f32[1,256]{1,0:T(1,128)S(1)}, f32[1,256]{1,0:T(1,128)}, u32[]{:S(2)}) copy-start(f32[1,256]{1,0:T(1,128)} %param.13) | copy-start | bytes 3076
  11.4 5.9 %copy-start.2 = (f32[1,64,1024]{2,1,0:T(8,128)S(1)}, f32[1,64,1024]{2,1,0:T(8,128)}, u32[]{:S(2)}) copy-start(f32[1,64,1024]{2,1,0:T(8,128)} %param.10) | copy-start | bytes 786436
  11.4 5.9 %copy-start.4 = (f32[1,64]{1,0:T(1,128)S(1)}, f32[1,64]{1,0:T(1,128)}, u32[]{:S(2)}) copy-start(f32[1,64]{1,0:T(1,128)} %param.12) | copy-start | bytes 772
  127.2 3.5 %slice-start = ((s8[4718592]{0:T(1024)(128)(4,1)}), s8[524288]{0:T(1024)(128)(4,1)S(1)}, s32[]{:S(2)}) async-start(s8[4718592]{0:T(1024)(128)(4,1)} %bitcast.27), calls=%async_computation.5 | async-start | bytes 1048576
  127.2 2.3 %slice-start.2 = ((f32[16,72,1024]{2,1,0:T(8,128)}), f32[16,64,1024]{2,1,0:T(8,128)S(1)}, s32[]{:S(2)}) async-start(f32[16,72,1024]{2,1,0:T(8,128)} %all-gather.3.cloned.1.call-done), calls=%async_computation.7 | async-start | bytes 8388608 | tf_op jit(solution)/shard_map/slice | solution.py:112
  127.2 3.6 %slice-start.1 = ((s8[4718592]{0:T(1024)(128)(4,1)}), s8[4194304]{0:T(1024)(128)(4,1)S(1)}, s32[]{:S(2)}) async-start(s8[4718592]{0:T(1024)(128)(4,1)} %bitcast.27), calls=%async_computation.6 | async-start | bytes 8388608
  159.7 5.2 %copy-start.1 = (f32[8,64,256]{2,1,0:T(8,128)}, f32[8,64,256]{2,1,0:T(8,128)S(1)}, u32[]{:S(2)}) copy-start(f32[8,64,256]{2,1,0:T(8,128)S(1)} %all_to_all.23.mine_ref) | copy-start | bytes 1572868
  159.7 5.2 %collective-permute-start.1 = (f32[8,64,256]{2,1,0:T(8,128)S(1)}, f32[8,64,256]{2,1,0:T(8,128)S(1)}, u32[]{:S(2)}, u32[]{:S(2)}) collective-permute-start(f32[8,64,256]{2,1,0:T(8,128)S(1)} %all_to_all.23.mine_ref), channel_id=1, source_target_pairs={{0,16},{16,0},{1,17},{17,1},{2,18},{18,2},{3,19},{19,3},{4,20},{20... | collective-permute-start | bytes 1572872 | tf_op jit(solution)/shard_map/ppermute | solution.py:133
  164.9 0.8 copy-start.3
Sparse Core Ops, SparseCore 0:
  18.4 64.0 all-gather.2

commit v3 on v2

v3 whole, which is shorter than its diff:
```python
import functools

import jax
import jax.numpy as jnp
from jax import lax
from jax.experimental import pallas as pl
from jax.experimental.pallas import tpu as pltpu
from jax.sharding import Mesh, PartitionSpec as P

DAMPING = 0.001
LIMIT = float(2**17 - 2)
VALUE_UNIT = float(2**33)
GRP = ("x", "yl", "core")
WK = ("z", "yh")
HIGH = lax.Precision.HIGH
PACK_GRANT = 59 * 2**20
MIDDLE_GRANT = 24 * 2**20
ENCODE_GRANT = 24 * 2**20


def pack_kernel(owned_ref, wide_ref, narrow_ref, out_ref, stage_ref, load_sems, store_sems):
    layers, _, wide = wide_ref.shape
    narrow = narrow_ref.shape[2]
    loads, stores = [], []
    for group in range(layers):
        layer = owned_ref[group]
        stage = stage_ref.at[group]
        loads.append(
            (
                pltpu.make_async_copy(
                    wide_ref.at[layer], stage.at[:, pl.ds(0, wide)], load_sems.at[group, 0]
                ),
                pltpu.make_async_copy(
                    narrow_ref.at[layer], stage.at[:, pl.ds(wide, narrow)], load_sems.at[group, 1]
                ),
            )
        )
        stores.append(pltpu.make_async_copy(stage, out_ref.at[group], store_sems.at[group]))
    for pair in loads:
        pair[0].start()
        pair[1].start()
    for pair, store in zip(loads, stores):
        pair[0].wait()
        pair[1].wait()
        store.start()
    for store in stores:
        store.wait()


def pack_tokens(owned_layer, wide_side, narrow_side):
    layers, tokens, wide = wide_side.shape
    narrow = narrow_side.shape[2]
    packed = (layers, tokens, wide + narrow)
    return pl.pallas_call(
        pack_kernel,
        out_shape=jax.ShapeDtypeStruct(packed, wide_side.dtype),
        in_specs=[
            pl.BlockSpec(memory_space=pltpu.SMEM),
            pl.BlockSpec(memory_space=pl.ANY),
            pl.BlockSpec(memory_space=pl.ANY),
        ],
        out_specs=pl.BlockSpec(memory_space=pl.ANY),
        scratch_shapes=[
            pltpu.VMEM(packed, wide_side.dtype),
            pltpu.SemaphoreType.DMA((layers, 2)),
            pltpu.SemaphoreType.DMA((layers,)),
        ],
        compiler_params=pltpu.CompilerParams(vmem_limit_bytes=PACK_GRANT),
    )(owned_layer, wide_side, narrow_side)


def place_kernel(owned_ref, core_ref, mine_ref, other_ref, out_ref, sems):
    core = core_ref[0]
    chips = mine_ref.shape[0]
    copies = []
    for chip in range(chips):
        copies.append(
            pltpu.make_async_copy(
                mine_ref.at[chip], out_ref.at[owned_ref[2 * chip + core]], sems.at[chip, 0]
            )
        )
        copies.append(
            pltpu.make_async_copy(
                other_ref.at[chip], out_ref.at[owned_ref[2 * chip + 1 - core]], sems.at[chip, 1]
            )
        )
    for copy in copies:
        copy.start()
    for copy in copies:
        copy.wait()


def place(owned_layer, core, mine, other):
    chips, rows, narrow = mine.shape
    return pl.pallas_call(
        place_kernel,
        out_shape=jax.ShapeDtypeStruct((2 * chips, rows, narrow), mine.dtype),
        in_specs=[
            pl.BlockSpec(memory_space=pltpu.SMEM),
            pl.BlockSpec(memory_space=pltpu.SMEM),
            pl.BlockSpec(memory_space=pltpu.VMEM),
            pl.BlockSpec(memory_space=pltpu.VMEM),
        ],
        out_specs=pl.BlockSpec(memory_space=pl.ANY),
        scratch_shapes=[pltpu.SemaphoreType.DMA((chips, 2))],
        compiler_params=pltpu.CompilerParams(vmem_limit_bytes=4 * 2**20),
    )(owned_layer, core, mine, other)


def split(value):
    high = value.astype(jnp.bfloat16)
    return high, (value - high.astype(jnp.float32)).astype(jnp.bfloat16)


def product(value, high, low, contract):
    rows = value.shape[0]
    dims = (((1,), (contract,)), ((), ()))
    value_high, value_low = split(value)
    both = lax.dot_general(
        jnp.concatenate([value_high, value_low], axis=0), high, dims,
        preferred_element_type=jnp.float32,
    )
    rest = lax.dot_general(value_high, low, dims, preferred_element_type=jnp.float32)
    return both[:rows] + both[rows:] + rest


def encode_kernel(sums_ref, small_ref, values_ref, held_ref, out_ref, basis_ref, sem):
    load = pltpu.make_async_copy(held_ref, basis_ref, sem)
    load.start()
    workers = out_ref.shape[0]
    narrow = small_ref.shape[1]
    rows = narrow // workers
    half = rows // 2
    tiles = sums_ref.shape[1] // 128
    base = tiles * half
    lane = lax.broadcasted_iota(jnp.int32, (half, 128), 1)
    values = (values_ref[...] * VALUE_UNIT).astype(jnp.int32)
    values = jnp.concatenate([values, jnp.zeros_like(values)], axis=1)
    values = jnp.broadcast_to(values, (half, 128))
    high, low_part = split(sums_ref[...])
    parts = product(small_ref[0].T, high, low_part, 0)
    for worker in range(workers):
        part = parts[worker * rows : (worker + 1) * rows, :]
        most = jnp.max(jnp.abs(part), axis=1, keepdims=True)
        power = jnp.ceil(jnp.log2(jnp.maximum(most, 2.0**-125)))
        code = jnp.floor(part * (jnp.exp2(-power) * LIMIT) + 0.5).astype(jnp.int32)
        low = jnp.zeros((half, 128), jnp.int32)
        for tile in range(tiles):
            piece = code[:, tile * 128 : (tile + 1) * 128]
            first, second = piece[:half], piece[half:]
            out_ref[worker, tile * half : (tile + 1) * half, :] = ((first >> 2) << 16) | (
                (second >> 2) & 0xFFFF
            )
            low = low | ((first & 3) << (4 * tile)) | ((second & 3) << (4 * tile + 2))
        out_ref[worker, base : base + half, :] = low
        power = power.astype(jnp.int32)
        out_ref[worker, base + half :, :] = jnp.where(
            lane < 64, values, jnp.where(lane < 96, power[:half], power[half:])
        )
    load.wait()


def encode(sums, narrow_basis, wide_values, held, workers):
    narrow, wide = sums.shape
    words = (narrow // workers // 2) * (wide // 128 + 2)
    return pl.pallas_call(
        encode_kernel,
        out_shape=(
            jax.ShapeDtypeStruct((workers, words, 128), jnp.int32),
            jax.ShapeDtypeStruct(held.shape, held.dtype),
        ),
        in_specs=[pl.BlockSpec(memory_space=pltpu.VMEM)] * 3 + [pl.BlockSpec(memory_space=pl.ANY)],
        out_specs=(pl.BlockSpec(memory_space=pltpu.VMEM), pl.BlockSpec(memory_space=pltpu.VMEM)),
        scratch_shapes=[pltpu.SemaphoreType.DMA],
        compiler_params=pltpu.CompilerParams(vmem_limit_bytes=ENCODE_GRANT),
    )(sums, narrow_basis, wide_values, held)


def middle_kernel(total_tokens, worker_ref, coded_ref, basis_ref, small_ref, out_ref):
    workers, words, _ = coded_ref.shape
    half = 8
    tiles = words // half - 2
    base = tiles * half
    lane = lax.broadcasted_iota(jnp.int32, (half, 128), 1)
    sums = [[jnp.zeros((half, 128), jnp.float32) for _ in range(tiles)] for _ in range(2)]
    values = []
    for worker in range(workers):
        tail = coded_ref[worker, base + half :, :]
        values.append(tail.astype(jnp.float32) * (1.0 / VALUE_UNIT))
        units = [
            jnp.exp2(tail[:, at : at + 1].astype(jnp.float32)) * (1.0 / LIMIT) for at in (64, 96)
        ]
        low = coded_ref[worker, base : base + half, :]
        for tile in range(tiles):
            word = coded_ref[worker, tile * half : (tile + 1) * half, :]
            first = ((word >> 16) << 2) | ((low >> (4 * tile)) & 3)
            second = (((word << 16) >> 16) << 2) | ((low >> (4 * tile + 2)) & 3)
            sums[0][tile] += first.astype(jnp.float32) * units[0]
            sums[1][tile] += second.astype(jnp.float32) * units[1]
    gradient = jnp.concatenate(
        [jnp.concatenate(part, axis=1) for part in sums], axis=0
    ) * (1.0 / total_tokens)
    wide_values = jnp.concatenate(
        [
            jnp.where(lane < 64, values[2 * tile], pltpu.roll(values[2 * tile + 1], 64, 1))
            for tile in range(tiles)
        ],
        axis=1,
    )[:1]
    count = small_ref.shape[1]
    own = lax.broadcasted_iota(jnp.int32, (2 * half, count), 1) == (
        worker_ref[0] * (2 * half) + lax.broadcasted_iota(jnp.int32, (2 * half, count), 0)
    )
    small = jnp.sum(jnp.where(own, small_ref[...], 0.0), axis=1, keepdims=True)
    high, low = (
        jnp.concatenate(
            [basis_ref[z, h, i] for z in range(basis_ref.shape[0]) for h in range(basis_ref.shape[1])],
            axis=0,
        )
        for i in range(2)
    )
    rotated = product(gradient, high, low, 0)
    scaled = rotated / (small * wide_values + DAMPING)
    precond = product(scaled, high, low, 1)
    for tile in range(tiles):
        piece = precond[:, tile * 128 : (tile + 1) * 128]
        first, second = piece[:half], piece[half:]
        out_ref[2 * tile] = jnp.where(lane < 64, first, pltpu.roll(second, 64, 1))
        out_ref[2 * tile + 1] = jnp.where(lane < 64, pltpu.roll(first, 64, 1), second)


def middle(worker, coded, basis, narrow_values, total_tokens):
    return pl.pallas_call(
        functools.partial(middle_kernel, total_tokens),
        out_shape=jax.ShapeDtypeStruct((coded.shape[0], 8, 128), jnp.float32),
        in_specs=[pl.BlockSpec(memory_space=pltpu.SMEM)] + [pl.BlockSpec(memory_space=pltpu.VMEM)] * 3,
        out_specs=pl.BlockSpec(memory_space=pltpu.VMEM),
        compiler_params=pltpu.CompilerParams(vmem_limit_bytes=MIDDLE_GRANT),
    )(worker, coded, basis, narrow_values)


def last_kernel(precond_ref, small_ref, out_ref):
    pieces = []
    for worker in range(precond_ref.shape[0]):
        block = precond_ref[worker]
        pieces += [block[:, :64], block[:, 64:]]
    columns = jnp.concatenate(pieces, axis=0)
    mine = lax.dot_general(
        columns.T, small_ref[0], (((1,), (1,)), ((), ())),
        precision=lax.Precision.HIGHEST, preferred_element_type=jnp.float32,
    )
    for chip in range(out_ref.shape[0]):
        out_ref[chip] = mine


def last(precond, narrow_basis, chips):
    return pl.pallas_call(
        last_kernel,
        out_shape=jax.ShapeDtypeStruct((chips, 64, narrow_basis.shape[1]), jnp.float32),
        in_specs=[pl.BlockSpec(memory_space=pltpu.VMEM)] * 2,
        out_specs=pl.BlockSpec(memory_space=pltpu.VMEM),
        compiler_params=pltpu.CompilerParams(vmem_limit_bytes=4 * 2**20),
    )(precond, narrow_basis)


def local(
    owned_layer, wide_side, narrow_side, wide_basis, narrow_basis, wide_values, narrow_values
):
    groups = lax.axis_size(GRP)
    workers = lax.axis_size(WK)
    layers, tokens, wide = wide_side.shape
    narrow = narrow_side.shape[2]
    total_tokens = tokens * groups * workers

    swapped = lax.ppermute(wide_basis[0], "yh", [(0, 1), (1, 0)])
    packed = pack_tokens(owned_layer, wide_side, narrow_side)
    low = lax.axis_index("yh") == 0
    held = jnp.stack(
        [jnp.where(low, wide_basis[0], swapped), jnp.where(low, swapped, wide_basis[0])]
    )
    high = lax.reduce_precision(held, 8, 7)
    held = jnp.stack([high.astype(jnp.bfloat16), (held - high).astype(jnp.bfloat16)], axis=1)
    worker = lax.axis_index(WK).reshape(1)
    core = lax.axis_index("core").reshape(1)
    held, packed, worker, core = lax.optimization_barrier((held, packed, worker, core))
    held = lax.all_gather(held, "z", axis=0, tiled=False)

    packed = lax.all_to_all(packed, GRP, 0, 0, tiled=True)
    packed = packed.reshape(groups * tokens, wide + narrow)
    sums = lax.dot_general(
        packed[:, wide:], packed[:, :wide], (((0,), (0,)), ((), ())),
        preferred_element_type=jnp.float32,
    )
    coded, basis = encode(sums, narrow_basis, wide_values, held, workers)
    coded = lax.all_to_all(coded, WK, 0, 0, tiled=True)
    precond = middle(worker, coded, basis, narrow_values, total_tokens)
    precond = lax.all_to_all(precond, WK, 0, 0, tiled=True)
    spread = last(precond, narrow_basis, groups // 2)
    spread = lax.all_to_all(spread, ("x", "yl"), 0, 0, tiled=True)
    other = lax.ppermute(spread, "core", [(0, 1), (1, 0)])
    return place(owned_layer, core, spread, other)


def solution(mesh):
    fine = Mesh(
        mesh.devices.reshape(4, 2, 2, 8, 2), ("x", "yl", "core", "z", "yh")
    )
    return jax.shard_map(
        local,
        mesh=fine,
        in_specs=(
            P(),
            P(None, GRP + WK, None),
            P(None, GRP + WK, None),
            P(GRP, WK, None),
            P(GRP, None, None),
            P(GRP, WK),
            P(GRP, None),
        ),
        out_specs=P(None, WK, None),
        check_vma=False,
    )
```

time: 175 us -> 160 us (0.914)
  blocking collectives: 130 us -> 121 us
  matrix products: 5.84 us -> 1.26 us
  Pallas kernels: 8.13 us -> 11.5 us
  local copies, waits for them, and re-layouts: 5.01 us -> 2.2 us
  other arithmetic: 2.81 us -> 0.96 us
    all_to_all x2, blocking collectives: 51.8 us -> 43.2 us  [the longest x1 31.2 us: local(): coded = lax.all_to_all(coded, WK, 0, 0, tiled=True)]
    dot_general x4 -> x0, matrix products: 4.58 us -> none  [the longest x1 2.54 us: local(): lax.dot_general(scaled, basis, (((1,), (1,)), ((), ())), precision=HIGH)]
    pallas_call x1 -> x4, Pallas kernels: 5.83 us -> 9.87 us  [the longest x1 5.87 us: pack_tokens(): pl.pallas_call(pack_kernel, out_shape=jax.ShapeDtypeStruct(packed, wide_s...]
    slice x3 -> x0, local copies, waits for them, and re-layouts: 3.16 us -> none  [the longest x2 2.29 us: local(): basis = held[:, :rows].reshape(wide, wide)]
  transfers between devices with their start and end apart: 3 -> 3, of which waited for: 1 -> 1; matrix products, arithmetic and copies ran while one was open for 1% -> 1% of each run, Pallas kernels for 3% -> 4%
where the time goes in v3:
time: 160 us
  blocking collectives  121 us (76%)
  between operations  13.5 us (8%)
  Pallas kernels  11.5 us (7%)
  starting transfers between devices  7.75 us (5%)
  local copies, waits for them, and re-layouts  2.2 us (1%)
    all_to_all x1, blocking collectives, local(): packed = lax.all_to_all(packed, GRP, 0, 0, tiled=True)  67.1 us
    all_to_all x1, blocking collectives, local(): coded = lax.all_to_all(coded, WK, 0, 0, tiled=True)  31.2 us
    all_to_all x1, blocking collectives, local(): precond = lax.all_to_all(precond, WK, 0, 0, tiled=True)  12 us
    all_to_all x1, blocking collectives, local(): spread = lax.all_to_all(spread, ('x', 'yl'), 0, 0, tiled=True)  11 us
    pallas_call x1, Pallas kernels, pack_tokens(): pl.pallas_call(pack_kernel, out_shape=jax.ShapeDtypeStruct(packed, wide_s...  5.87 us
    ppermute x1, starting transfers between devices, local(): other = lax.ppermute(spread, 'core', [(0, 1), (1, 0)])  4 us
    ppermute x1, starting transfers between devices, local(): swapped = lax.ppermute(wide_basis[0], 'yh', [(0, 1), (1, 0)])  3.74 us
  transfers between devices with their start and end apart: 3, of which 1 were waited for; matrix products, arithmetic and copies ran while one was open for 1% of the time, Pallas kernels for 4%

profile of v3, /device:TPU:1, one launch (start us, length us, event | category | flops | bytes accessed | tf_op | source)
XLA Modules:
  0.0 160.1 jit_solution(16749477757738010018)
XLA Ops:
  6.5 0.0 all-gather.3.cloned.1.call-start
  6.5 3.7 %collective-permute-start = (f32[64,1024]{1,0:T(8,128)}, f32[64,1024]{1,0:T(8,128)S(1)}, u32[]{:S(2)}, u32[]{:S(2)}) collective-permute-start(f32[64,1024]{1,0:T(8,128)} %bitcast.13), channel_id=1, source_target_pairs={{0,1},{1,0},{2,3},{3,2},{4,5},{5,4},{6,7},{7,6},{8,9},{9,8},{10,11... | collective-permute-start | bytes 786440 | tf_op jit(solution)/shard_map/ppermute | solution.py:275
  10.3 5.9 %shard_map.73 = bf16[16,128,1280]{2,1,0:T(8,128)(2,1)} custom-call(s32[16]{0:T(128)} %owned_ref.3, bf16[16,128,1024]{2,1,0:T(8,128)(2,1)} %wide_ref.1, bf16[16,128,256]{2,1,0:T(8,128)(2,1)} %narrow_ref.1), custom_call_target="tpu_custom_call" | custom-call | tf_op jit(solution)/shard_map/pallas_call | solution.py:54
  16.2 0.0 collective-permute-done
  16.2 0.0 copy-done.5
  16.2 0.1 reduce-precision_convert_fusion
  16.3 0.8 pad_maximum_fusion.1
  17.2 0.0 all-gather.3.cloned.1.call-update
  17.2 67.1 %all_to_all.20 = bf16[16,128,1280]{2,1,0:T(8,128)(2,1)S(1)} all-to-all(bf16[16,128,1280]{2,1,0:T(8,128)(2,1)} %shard_map.73), channel_id=1, replica_groups=mesh['x'=4,'yl'=2,'core'=2,'z'=8,'yh'=2] {'x','yl','core'}, dimensions={0} | all-to-all | bytes 10485760 | tf_op jit(solution)/shard_map/all_to_all | solution.py:288
  84.3 1.3 fusion.sums_ref
  85.6 0.0 copy-start.3
  85.6 0.0 all-gather.3.cloned.1.call-done
  85.7 2.2 %copy-done = bf16[16,2,64,1024]{3,2,1,0:T(8,128)(2,1)S(1)} copy-done((bf16[16,2,64,1024]{3,2,1,0:T(8,128)(2,1)S(1)}, bf16[16,2,64,1024]{3,2,1,0:T(8,128)(2,1)}, u32[]{:S(2)}) %copy-start) | copy-done | bytes 4194328
  87.8 1.4 shard_map.74
  89.2 0.0 copy-start.2
  89.2 31.2 %all_to_all.21.coded_ref = s32[16,80,128]{2,1,0:T(8,128)S(1)} all-to-all(s32[16,80,128]{2,1,0:T(8,128)S(1)} %get-tuple-element.15), channel_id=1, replica_groups=mesh['x'=4,'yl'=2,'core'=2,'z'=8,'yh'=2] {'z','yh'}, dimensions={0} | all-to-all | bytes 1310720 | tf_op jit(solution)/shard_map/all_to_all | solution.py:295
  120.4 2.2 %shard_map.75 = f32[16,8,128]{2,1,0:T(8,128)S(1)} custom-call(s32[1]{0:T(128)} %bitcast.3.worker_ref, s32[16,80,128]{2,1,0:T(8,128)S(1)} %all_to_all.21.coded_ref, bf16[8,2,2,64,1024]{4,3,2,1,0:T(8,128)(2,1)S(1)} %get-tuple-element.16.basis_ref, f32[1,256]{1,0:T(1,128)S(1)} %copy-done.3), custom_call_target="tpu_custom_call" | custom-call | tf_op jit(solution)/shard_map/pallas_call | solution.py:233
  122.6 12.0 %all_to_all.22.precond_ref = f32[16,8,128]{2,1,0:T(8,128)S(1)} all-to-all(f32[16,8,128]{2,1,0:T(8,128)S(1)} %shard_map.75), channel_id=1, replica_groups=mesh['x'=4,'yl'=2,'core'=2,'z'=8,'yh'=2] {'z','yh'}, dimensions={0} | all-to-all | bytes 131072 | tf_op jit(solution)/shard_map/all_to_all | solution.py:297
  134.7 0.5 shard_map.76
  135.1 11.0 %all_to_all.23.mine_ref = f32[8,64,256]{2,1,0:T(8,128)S(1)} all-to-all(f32[8,64,256]{2,1,0:T(8,128)S(1)} %shard_map.76), channel_id=1, replica_groups=mesh['x'=4,'yl'=2,'core'=2,'z'=8,'yh'=2] {'x','yl'}, dimensions={0} | all-to-all | bytes 1048576 | tf_op jit(solution)/shard_map/all_to_all | solution.py:299
  146.1 4.0 %collective-permute-start.1 = (f32[8,64,256]{2,1,0:T(8,128)S(1)}, f32[8,64,256]{2,1,0:T(8,128)S(1)}, u32[]{:S(2)}, u32[]{:S(2)}) collective-permute-start(f32[8,64,256]{2,1,0:T(8,128)S(1)} %all_to_all.23.mine_ref), channel_id=1, source_target_pairs={{0,16},{16,0},{1,17},{17,1},{2,18},{18,2},{3,19},{19,3},{4,20},{20... | collective-permute-start | bytes 1572872 | tf_op jit(solution)/shard_map/ppermute | solution.py:300
  150.1 1.5 collective-permute-done.1.other_ref
  151.6 0.0 copy-done.2
  151.6 1.6 %shard_map.77 = f32[16,64,256]{2,1,0:T(8,128)} custom-call(s32[16]{0:T(128)S(1)} %copy-done.2, s32[1]{0:T(128)} %bitcast.4.core_ref, f32[8,64,256]{2,1,0:T(8,128)S(1)} %all_to_all.23.mine_ref, f32[8,64,256]{2,1,0:T(8,128)S(1)} %collective-permute-done.1.other_ref), custom_call_target="tpu_custom_call" | custom-call | tf_op jit(solution)/shard_map/pallas_call | solution.py:95
  (8 shorter events, 0.1 us)
Async XLA Ops:
  6.5 79.1 %all-gather.3.cloned.1.call-start = ((), (), s32[]{:S(2)}) async-start(), calls=%async_computation.4 | async-start | bytes 4718592 | tf_op jit(solution)/shard_map/all_gather | solution.py:286
  6.5 9.6 %collective-permute-start = (f32[64,1024]{1,0:T(8,128)}, f32[64,1024]{1,0:T(8,128)S(1)}, u32[]{:S(2)}, u32[]{:S(2)}) collective-permute-start(f32[64,1024]{1,0:T(8,128)} %bitcast.13), channel_id=1, source_target_pairs={{0,1},{1,0},{2,3},{3,2},{4,5},{5,4},{6,7},{7,6},{8,9},{9,8},{10,11... | collective-permute-start | bytes 786440 | tf_op jit(solution)/shard_map/ppermute | solution.py:275
  10.3 5.9 %copy-start.5 = (f32[1,64,1024]{2,1,0:T(8,128)S(1)}, f32[1,64,1024]{2,1,0:T(8,128)}, u32[]{:S(2)}) copy-start(f32[1,64,1024]{2,1,0:T(8,128)} %param.10) | copy-start | bytes 786436
  84.3 1.3 copy-start.1
  84.3 1.3 copy-start.4
  85.6 34.8 %copy-start.3 = (f32[1,256]{1,0:T(1,128)S(1)}, f32[1,256]{1,0:T(1,128)}, u32[]{:S(2)}) copy-start(f32[1,256]{1,0:T(1,128)} %small_ref.4) | copy-start | bytes 3076
  85.7 2.2 %copy-start = (bf16[16,2,64,1024]{3,2,1,0:T(8,128)(2,1)S(1)}, bf16[16,2,64,1024]{3,2,1,0:T(8,128)(2,1)}, u32[]{:S(2)}) copy-start(bf16[16,2,64,1024]{3,2,1,0:T(8,128)(2,1)} %all-gather.3.cloned.1.call-done) | copy-start | bytes 12582916
  89.2 62.4 %copy-start.2 = (s32[16]{0:T(128)S(1)}, s32[16]{0:T(128)}, u32[]{:S(2)}) copy-start(s32[16]{0:T(128)} %owned_ref.3) | copy-start | bytes 196
  146.1 5.5 %collective-permute-start.1 = (f32[8,64,256]{2,1,0:T(8,128)S(1)}, f32[8,64,256]{2,1,0:T(8,128)S(1)}, u32[]{:S(2)}, u32[]{:S(2)}) collective-permute-start(f32[8,64,256]{2,1,0:T(8,128)S(1)} %all_to_all.23.mine_ref), channel_id=1, source_target_pairs={{0,16},{16,0},{1,17},{17,1},{2,18},{18,2},{3,19},{19,3},{4,20},{20... | collective-permute-start | bytes 1572872 | tf_op jit(solution)/shard_map/ppermute | solution.py:300
Sparse Core Ops, SparseCore 0:
  17.3 58.7 all-gather.2

commit v4 on v3

--- a/solution.py
+++ b/solution.py
@@ -13,9 +13,10 @@
 GRP = ("x", "yl", "core")
 WK = ("z", "yh")
 HIGH = lax.Precision.HIGH
+PLACE_GRANT = 4 * 2**20
 PACK_GRANT = 59 * 2**20
 MIDDLE_GRANT = 24 * 2**20
-ENCODE_GRANT = 24 * 2**20
+ENCODE_GRANT = 47 * 2**20
 
 
 def pack_kernel(owned_ref, wide_ref, narrow_ref, out_ref, stage_ref, load_sems, store_sems):
@@ -69,42 +70,38 @@
     )(owned_layer, wide_side, narrow_side)
 
 
-def place_kernel(owned_ref, core_ref, mine_ref, other_ref, out_ref, sems):
-    core = core_ref[0]
-    chips = mine_ref.shape[0]
-    copies = []
-    for chip in range(chips):
-        copies.append(
-            pltpu.make_async_copy(
-                mine_ref.at[chip], out_ref.at[owned_ref[2 * chip + core]], sems.at[chip, 0]
-            )
+def place_kernel(owned_ref, which_ref, blocks_ref, *rest):
+    out_ref, sems = rest[-2:]
+    which = which_ref[0]
+    copies = [
+        pltpu.make_async_copy(
+            blocks_ref.at[chip], out_ref.at[owned_ref[2 * chip + which]], sems.at[chip]
         )
-        copies.append(
-            pltpu.make_async_copy(
-                other_ref.at[chip], out_ref.at[owned_ref[2 * chip + 1 - core]], sems.at[chip, 1]
-            )
-        )
+        for chip in range(blocks_ref.shape[0])
+    ]
     for copy in copies:
         copy.start()
     for copy in copies:
         copy.wait()
 
 
-def place(owned_layer, core, mine, other):
-    chips, rows, narrow = mine.shape
+def place(owned_layer, which, blocks, into=None):
+    chips, rows, narrow = blocks.shape
+    more = () if into is None else (into,)
     return pl.pallas_call(
         place_kernel,
-        out_shape=jax.ShapeDtypeStruct((2 * chips, rows, narrow), mine.dtype),
+        out_shape=jax.ShapeDtypeStruct((2 * chips, rows, narrow), blocks.dtype),
         in_specs=[
             pl.BlockSpec(memory_space=pltpu.SMEM),
             pl.BlockSpec(memory_space=pltpu.SMEM),
             pl.BlockSpec(memory_space=pltpu.VMEM),
-            pl.BlockSpec(memory_space=pltpu.VMEM),
-        ],
+        ]
+        + [pl.BlockSpec(memory_space=pl.ANY)] * len(more),
         out_specs=pl.BlockSpec(memory_space=pl.ANY),
-        scratch_shapes=[pltpu.SemaphoreType.DMA((chips, 2))],
-        compiler_params=pltpu.CompilerParams(vmem_limit_bytes=4 * 2**20),
-    )(owned_layer, core, mine, other)
+        input_output_aliases={3: 0} if more else {},
+        scratch_shapes=[pltpu.SemaphoreType.DMA((chips,))],
+        compiler_params=pltpu.CompilerParams(vmem_limit_bytes=PLACE_GRANT),
+    )(owned_layer, which, blocks, *more)
 
 
 def split(value):
@@ -124,9 +121,13 @@
     return both[:rows] + both[rows:] + rest
 
 
-def encode_kernel(sums_ref, small_ref, values_ref, held_ref, out_ref, basis_ref, sem):
-    load = pltpu.make_async_copy(held_ref, basis_ref, sem)
-    load.start()
+def encode_kernel(sums_ref, small_ref, values_ref, held_ref, out_ref, basis_ref, sems):
+    loads = [
+        pltpu.make_async_copy(held_ref.at[z], basis_ref.at[z], sems.at[z])
+        for z in range(held_ref.shape[0])
+    ]
+    for load in loads:
+        load.start()
     workers = out_ref.shape[0]
     narrow = small_ref.shape[1]
     rows = narrow // workers
@@ -157,7 +158,8 @@
         out_ref[worker, base + half :, :] = jnp.where(
             lane < 64, values, jnp.where(lane < 96, power[:half], power[half:])
         )
-    load.wait()
+    for load in loads:
+        load.wait()
 
 
 def encode(sums, narrow_basis, wide_values, held, workers):
@@ -171,7 +173,7 @@
         ),
         in_specs=[pl.BlockSpec(memory_space=pltpu.VMEM)] * 3 + [pl.BlockSpec(memory_space=pl.ANY)],
         out_specs=(pl.BlockSpec(memory_space=pltpu.VMEM), pl.BlockSpec(memory_space=pltpu.VMEM)),
-        scratch_shapes=[pltpu.SemaphoreType.DMA],
+        scratch_shapes=[pltpu.SemaphoreType.DMA((held.shape[0],))],
         compiler_params=pltpu.CompilerParams(vmem_limit_bytes=ENCODE_GRANT),
     )(sums, narrow_basis, wide_values, held)
 
@@ -298,7 +300,8 @@
     spread = last(precond, narrow_basis, groups // 2)
     spread = lax.all_to_all(spread, ("x", "yl"), 0, 0, tiled=True)
     other = lax.ppermute(spread, "core", [(0, 1), (1, 0)])
-    return place(owned_layer, core, spread, other)
+    placed = place(owned_layer, core, spread)
+    return place(owned_layer, 1 - core, other, placed)
 
 
 def solution(mesh):

time: 160 us -> 159 us (level)
  Pallas kernels: 11.5 us -> 13.9 us
  local copies, waits for them, and re-layouts: 2.2 us -> 0.02 us
    unnamed x12 -> x10, local copies, waits for them, and re-layouts: 2.2 us -> 0.02 us
  transfers between devices with their start and end apart: 3 -> 3, of which waited for: 1 -> 1; matrix products, arithmetic and copies ran while one was open for 1% -> 1% of each run, Pallas kernels for 4% -> 5%
where the time goes in v4:
time: 159 us
  blocking collectives  121 us (76%)
  Pallas kernels  13.9 us (9%)
  between operations  13.5 us (8%)
  starting transfers between devices  7.76 us (5%)
    all_to_all x1, blocking collectives, local(): packed = lax.all_to_all(packed, GRP, 0, 0, tiled=True)  67.2 us
    all_to_all x1, blocking collectives, local(): coded = lax.all_to_all(coded, WK, 0, 0, tiled=True)  31.2 us
    all_to_all x1, blocking collectives, local(): precond = lax.all_to_all(precond, WK, 0, 0, tiled=True)  12 us
    all_to_all x1, blocking collectives, local(): spread = lax.all_to_all(spread, ('x', 'yl'), 0, 0, tiled=True)  11 us
    pallas_call x1, Pallas kernels, pack_tokens(): pl.pallas_call(pack_kernel, out_shape=jax.ShapeDtypeStruct(packed, wide_s...  5.86 us
    ppermute x1, starting transfers between devices, local(): other = lax.ppermute(spread, 'core', [(0, 1), (1, 0)])  4.01 us
    ppermute x1, starting transfers between devices, local(): swapped = lax.ppermute(wide_basis[0], 'yh', [(0, 1), (1, 0)])  3.74 us
  transfers between devices with their start and end apart: 3, of which 1 were waited for; matrix products, arithmetic and copies ran while one was open for 1% of the time, Pallas kernels for 5%

profile of v4, /device:TPU:1, one launch (start us, length us, event | category | flops | bytes accessed | tf_op | source)
XLA Modules:
  0.0 159.0 jit_solution(2441490784356730074)
XLA Ops:
  6.5 0.0 all-gather.3.cloned.1.call-start
  6.5 3.7 %collective-permute-start = (f32[64,1024]{1,0:T(8,128)}, f32[64,1024]{1,0:T(8,128)S(1)}, u32[]{:S(2)}, u32[]{:S(2)}) collective-permute-start(f32[64,1024]{1,0:T(8,128)} %bitcast.13), channel_id=1, source_target_pairs={{0,1},{1,0},{2,3},{3,2},{4,5},{5,4},{6,7},{7,6},{8,9},{9,8},{10,11... | collective-permute-start | bytes 786440 | tf_op jit(solution)/shard_map/ppermute | solution.py:277
  10.3 5.9 %shard_map.73 = bf16[16,128,1280]{2,1,0:T(8,128)(2,1)} custom-call(s32[16]{0:T(128)} %owned_ref.5, bf16[16,128,1024]{2,1,0:T(8,128)(2,1)} %wide_ref.1, bf16[16,128,256]{2,1,0:T(8,128)(2,1)} %narrow_ref.1), custom_call_target="tpu_custom_call" | custom-call | tf_op jit(solution)/shard_map/pallas_call | solution.py:55
  16.1 0.0 collective-permute-done
  16.2 0.0 copy-done.4
  16.2 0.1 reduce-precision_convert_fusion
  16.3 0.8 pad_maximum_fusion.1
  17.1 0.0 all-gather.3.cloned.1.call-update
  17.2 67.2 %all_to_all.20 = bf16[16,128,1280]{2,1,0:T(8,128)(2,1)S(1)} all-to-all(bf16[16,128,1280]{2,1,0:T(8,128)(2,1)} %shard_map.73), channel_id=1, replica_groups=mesh['x'=4,'yl'=2,'core'=2,'z'=8,'yh'=2] {'x','yl','core'}, dimensions={0} | all-to-all | bytes 10485760 | tf_op jit(solution)/shard_map/all_to_all | solution.py:290
  84.3 1.3 fusion.sums_ref
  85.6 0.0 copy-start.2
  85.6 0.0 all-gather.3.cloned.1.call-done
  85.7 2.6 %shard_map.74 = (s32[16,80,128]{2,1,0:T(8,128)S(1)}, bf16[8,2,2,64,1024]{4,3,2,1,0:T(8,128)(2,1)S(1)}) custom-call(f32[256,1024]{1,0:T(8,128)S(1)} %fusion.sums_ref, f32[1,256,256]{2,1,0:T(8,128)S(1)} %copy-done, f32[1,64]{1,0:T(1,128)S(1)} %copy-done.3, bf16[8,2,2,64,1024]{4,3,2,1,0:T(8,128)(2,1)} %bitcast.12), custom_call_target="tpu_custom_call" | custom-call | tf_op jit(solution)/shard_map/pallas_call | solution.py:168
  88.3 0.0 copy-start.1
  88.3 31.2 %all_to_all.21.coded_ref = s32[16,80,128]{2,1,0:T(8,128)S(1)} all-to-all(s32[16,80,128]{2,1,0:T(8,128)S(1)} %get-tuple-element.15), channel_id=1, replica_groups=mesh['x'=4,'yl'=2,'core'=2,'z'=8,'yh'=2] {'z','yh'}, dimensions={0} | all-to-all | bytes 1310720 | tf_op jit(solution)/shard_map/all_to_all | solution.py:297
  119.5 2.2 %shard_map.75 = f32[16,8,128]{2,1,0:T(8,128)S(1)} custom-call(s32[1]{0:T(128)} %bitcast.3.worker_ref, s32[16,80,128]{2,1,0:T(8,128)S(1)} %all_to_all.21.coded_ref, bf16[8,2,2,64,1024]{4,3,2,1,0:T(8,128)(2,1)S(1)} %get-tuple-element.16.basis_ref, f32[1,256]{1,0:T(1,128)S(1)} %copy-done.2), custom_call_target="tpu_custom_call" | custom-call | tf_op jit(solution)/shard_map/pallas_call | solution.py:235
  121.7 12.0 %all_to_all.22.precond_ref = f32[16,8,128]{2,1,0:T(8,128)S(1)} all-to-all(f32[16,8,128]{2,1,0:T(8,128)S(1)} %shard_map.75), channel_id=1, replica_groups=mesh['x'=4,'yl'=2,'core'=2,'z'=8,'yh'=2] {'z','yh'}, dimensions={0} | all-to-all | bytes 131072 | tf_op jit(solution)/shard_map/all_to_all | solution.py:299
  133.7 0.5 shard_map.76
  134.2 11.0 %all_to_all.23.blocks_ref = f32[8,64,256]{2,1,0:T(8,128)S(1)} all-to-all(f32[8,64,256]{2,1,0:T(8,128)S(1)} %shard_map.76), channel_id=1, replica_groups=mesh['x'=4,'yl'=2,'core'=2,'z'=8,'yh'=2] {'x','yl'}, dimensions={0} | all-to-all | bytes 1048576 | tf_op jit(solution)/shard_map/all_to_all | solution.py:301
  145.2 4.0 %collective-permute-start.1 = (f32[8,64,256]{2,1,0:T(8,128)S(1)}, f32[8,64,256]{2,1,0:T(8,128)S(1)}, u32[]{:S(2)}, u32[]{:S(2)}) collective-permute-start(f32[8,64,256]{2,1,0:T(8,128)S(1)} %all_to_all.23.blocks_ref), channel_id=1, source_target_pairs={{0,16},{16,0},{1,17},{17,1},{2,18},{18,2},{3,19},{19,3},{4,20},{20... | collective-permute-start | bytes 1572872 | tf_op jit(solution)/shard_map/ppermute | solution.py:302
  149.2 0.0 copy-done.1
  149.2 1.4 shard_map.77.rest_0_
  150.6 0.1 collective-permute-done.1.blocks_ref
  150.7 1.4 shard_map.78
  (7 shorter events, 0.1 us)
Async XLA Ops:
  6.5 79.1 %all-gather.3.cloned.1.call-start = ((), (), s32[]{:S(2)}) async-start(), calls=%async_computation.4 | async-start | bytes 4718592 | tf_op jit(solution)/shard_map/all_gather | solution.py:288
  6.5 9.6 %collective-permute-start = (f32[64,1024]{1,0:T(8,128)}, f32[64,1024]{1,0:T(8,128)S(1)}, u32[]{:S(2)}, u32[]{:S(2)}) collective-permute-start(f32[64,1024]{1,0:T(8,128)} %bitcast.13), channel_id=1, source_target_pairs={{0,1},{1,0},{2,3},{3,2},{4,5},{5,4},{6,7},{7,6},{8,9},{9,8},{10,11... | collective-permute-start | bytes 786440 | tf_op jit(solution)/shard_map/ppermute | solution.py:277
  10.3 5.9 %copy-start.4 = (f32[1,64,1024]{2,1,0:T(8,128)S(1)}, f32[1,64,1024]{2,1,0:T(8,128)}, u32[]{:S(2)}) copy-start(f32[1,64,1024]{2,1,0:T(8,128)} %param.10) | copy-start | bytes 786436
  84.3 1.3 copy-start
  84.3 1.3 copy-start.3
  85.6 33.9 %copy-start.2 = (f32[1,256]{1,0:T(1,128)S(1)}, f32[1,256]{1,0:T(1,128)}, u32[]{:S(2)}) copy-start(f32[1,256]{1,0:T(1,128)} %small_ref.4) | copy-start | bytes 3076
  88.3 60.9 %copy-start.1 = (s32[16]{0:T(128)S(1)}, s32[16]{0:T(128)}, u32[]{:S(2)}) copy-start(s32[16]{0:T(128)} %owned_ref.5) | copy-start | bytes 196
  145.2 5.5 %collective-permute-start.1 = (f32[8,64,256]{2,1,0:T(8,128)S(1)}, f32[8,64,256]{2,1,0:T(8,128)S(1)}, u32[]{:S(2)}, u32[]{:S(2)}) collective-permute-start(f32[8,64,256]{2,1,0:T(8,128)S(1)} %all_to_all.23.blocks_ref), channel_id=1, source_target_pairs={{0,16},{16,0},{1,17},{17,1},{2,18},{18,2},{3,19},{19,3},{4,20},{20... | collective-permute-start | bytes 1572872 | tf_op jit(solution)/shard_map/ppermute | solution.py:302
Sparse Core Ops, SparseCore 0:
  17.3 58.7 all-gather.2

commit v5 on v4

--- a/solution.py
+++ b/solution.py
@@ -8,7 +8,8 @@
 from jax.sharding import Mesh, PartitionSpec as P
 
 DAMPING = 0.001
-LIMIT = float(2**17 - 2)
+LIMIT = float(2**16 - 1)
+POWER_BIAS = 512
 VALUE_UNIT = float(2**33)
 GRP = ("x", "yl", "core")
 WK = ("z", "yh")
@@ -138,33 +139,33 @@
     values = (values_ref[...] * VALUE_UNIT).astype(jnp.int32)
     values = jnp.concatenate([values, jnp.zeros_like(values)], axis=1)
     values = jnp.broadcast_to(values, (half, 128))
+    sublane = lax.broadcasted_iota(jnp.int32, (half, 128), 0)
+    values = jnp.where(sublane < half // 2, values >> 15, values & 0x7FFF)
     high, low_part = split(sums_ref[...])
     parts = product(small_ref[0].T, high, low_part, 0)
     for worker in range(workers):
         part = parts[worker * rows : (worker + 1) * rows, :]
         most = jnp.max(jnp.abs(part), axis=1, keepdims=True)
-        power = jnp.ceil(jnp.log2(jnp.maximum(most, 2.0**-125)))
-        code = jnp.floor(part * (jnp.exp2(-power) * LIMIT) + 0.5).astype(jnp.int32)
+        power = jnp.ceil(jnp.log2(jnp.maximum(most, 2.0**-120)))
+        code = jnp.floor(part * jnp.exp2(-power) * LIMIT + 0.5).astype(jnp.int32)
         low = jnp.zeros((half, 128), jnp.int32)
         for tile in range(tiles):
             piece = code[:, tile * 128 : (tile + 1) * 128]
             first, second = piece[:half], piece[half:]
-            out_ref[worker, tile * half : (tile + 1) * half, :] = ((first >> 2) << 16) | (
-                (second >> 2) & 0xFFFF
+            out_ref[worker, tile * half : (tile + 1) * half, :] = ((first >> 1) << 16) | (
+                (second >> 1) & 0xFFFF
             )
-            low = low | ((first & 3) << (4 * tile)) | ((second & 3) << (4 * tile + 2))
-        out_ref[worker, base : base + half, :] = low
-        power = power.astype(jnp.int32)
-        out_ref[worker, base + half :, :] = jnp.where(
-            lane < 64, values, jnp.where(lane < 96, power[:half], power[half:])
-        )
+            low = low | ((first & 1) << (2 * tile)) | ((second & 1) << (2 * tile + 1))
+        power = power.astype(jnp.int32) + POWER_BIAS
+        more = jnp.where(lane < 64, values, jnp.where(lane < 96, power[:half], power[half:]))
+        out_ref[worker, base:, :] = low | (more << 16)
     for load in loads:
         load.wait()
 
 
 def encode(sums, narrow_basis, wide_values, held, workers):
     narrow, wide = sums.shape
-    words = (narrow // workers // 2) * (wide // 128 + 2)
+    words = (narrow // workers // 2) * (wide // 128 + 1)
     return pl.pallas_call(
         encode_kernel,
         out_shape=(
@@ -181,27 +182,26 @@
 def middle_kernel(total_tokens, worker_ref, coded_ref, basis_ref, small_ref, out_ref):
     workers, words, _ = coded_ref.shape
     half = 8
-    tiles = words // half - 2
+    tiles = words // half - 1
     base = tiles * half
     lane = lax.broadcasted_iota(jnp.int32, (half, 128), 1)
     sums = [[jnp.zeros((half, 128), jnp.float32) for _ in range(tiles)] for _ in range(2)]
     values = []
     for worker in range(workers):
-        tail = coded_ref[worker, base + half :, :]
-        values.append(tail.astype(jnp.float32) * (1.0 / VALUE_UNIT))
-        units = [
-            jnp.exp2(tail[:, at : at + 1].astype(jnp.float32)) * (1.0 / LIMIT) for at in (64, 96)
-        ]
-        low = coded_ref[worker, base : base + half, :]
+        low = coded_ref[worker, base:, :]
+        tail = ((low >> 16) & 0xFFFF).astype(jnp.float32)
+        value = tail[:1] * 2.0**15 + tail[half // 2 : half // 2 + 1]
+        values.append(jnp.broadcast_to(value * (1.0 / VALUE_UNIT), (half, 128)))
+        units = [jnp.exp2(tail[:, at : at + 1] - POWER_BIAS) for at in (64, 96)]
         for tile in range(tiles):
             word = coded_ref[worker, tile * half : (tile + 1) * half, :]
-            first = ((word >> 16) << 2) | ((low >> (4 * tile)) & 3)
-            second = (((word << 16) >> 16) << 2) | ((low >> (4 * tile + 2)) & 3)
+            first = ((word >> 16) << 1) | ((low >> (2 * tile)) & 1)
+            second = (((word << 16) >> 16) << 1) | ((low >> (2 * tile + 1)) & 1)
             sums[0][tile] += first.astype(jnp.float32) * units[0]
             sums[1][tile] += second.astype(jnp.float32) * units[1]
     gradient = jnp.concatenate(
         [jnp.concatenate(part, axis=1) for part in sums], axis=0
-    ) * (1.0 / total_tokens)
+    ) * (1.0 / (LIMIT * total_tokens))
     wide_values = jnp.concatenate(
         [
             jnp.where(lane < 64, values[2 * tile], pltpu.roll(values[2 * tile + 1], 64, 1))

time: 159 us -> 158 us (level)
    all_to_all x1, blocking collectives: 31.2 us -> 29.2 us  [local(): coded = lax.all_to_all(coded, WK, 0, 0, tiled=True)]
where the time goes in v5:
time: 158 us
  blocking collectives  120 us (76%)
  Pallas kernels  13.8 us (9%)
  between operations  13.5 us (9%)
  starting transfers between devices  7.87 us (5%)
    all_to_all x1, blocking collectives, local(): packed = lax.all_to_all(packed, GRP, 0, 0, tiled=True)  67.2 us
    all_to_all x1, blocking collectives, local(): coded = lax.all_to_all(coded, WK, 0, 0, tiled=True)  29.2 us
    all_to_all x1, blocking collectives, local(): precond = lax.all_to_all(precond, WK, 0, 0, tiled=True)  12.9 us
    all_to_all x1, blocking collectives, local(): spread = lax.all_to_all(spread, ('x', 'yl'), 0, 0, tiled=True)  10.7 us
    pallas_call x1, Pallas kernels, pack_tokens(): pl.pallas_call(pack_kernel, out_shape=jax.ShapeDtypeStruct(packed, wide_s...  5.86 us
    ppermute x1, starting transfers between devices, local(): other = lax.ppermute(spread, 'core', [(0, 1), (1, 0)])  4.12 us
    ppermute x1, starting transfers between devices, local(): swapped = lax.ppermute(wide_basis[0], 'yh', [(0, 1), (1, 0)])  3.74 us
  transfers between devices with their start and end apart: 3, of which 1 were waited for; matrix products, arithmetic and copies ran while one was open for 1% of the time, Pallas kernels for 5%

profile of v5, /device:TPU:1, one launch (start us, length us, event | category | flops | bytes accessed | tf_op | source)
XLA Modules:
  0.0 157.6 jit_solution(7437708400546027787)
XLA Ops:
  6.5 0.0 all-gather.3.cloned.1.call-start
  6.5 3.7 %collective-permute-start = (f32[64,1024]{1,0:T(8,128)}, f32[64,1024]{1,0:T(8,128)S(1)}, u32[]{:S(2)}, u32[]{:S(2)}) collective-permute-start(f32[64,1024]{1,0:T(8,128)} %bitcast.13), channel_id=1, source_target_pairs={{0,1},{1,0},{2,3},{3,2},{4,5},{5,4},{6,7},{7,6},{8,9},{9,8},{10,11... | collective-permute-start | bytes 786440 | tf_op jit(solution)/shard_map/ppermute | solution.py:277
  10.3 5.9 %shard_map.73 = bf16[16,128,1280]{2,1,0:T(8,128)(2,1)} custom-call(s32[16]{0:T(128)} %owned_ref.5, bf16[16,128,1024]{2,1,0:T(8,128)(2,1)} %wide_ref.1, bf16[16,128,256]{2,1,0:T(8,128)(2,1)} %narrow_ref.1), custom_call_target="tpu_custom_call" | custom-call | tf_op jit(solution)/shard_map/pallas_call | solution.py:56
  16.1 0.0 collective-permute-done
  16.2 0.0 copy-done.4
  16.2 0.1 reduce-precision_convert_fusion
  16.3 0.8 pad_maximum_fusion.1
  17.1 0.0 all-gather.3.cloned.1.call-update
  17.2 67.2 %all_to_all.20 = bf16[16,128,1280]{2,1,0:T(8,128)(2,1)S(1)} all-to-all(bf16[16,128,1280]{2,1,0:T(8,128)(2,1)} %shard_map.73), channel_id=1, replica_groups=mesh['x'=4,'yl'=2,'core'=2,'z'=8,'yh'=2] {'x','yl','core'}, dimensions={0} | all-to-all | bytes 10485760 | tf_op jit(solution)/shard_map/all_to_all | solution.py:290
  84.3 1.3 fusion.sums_ref
  85.6 0.0 copy-start.2
  85.6 0.0 all-gather.3.cloned.1.call-done
  85.7 2.5 %shard_map.74 = (s32[16,72,128]{2,1,0:T(8,128)S(1)}, bf16[8,2,2,64,1024]{4,3,2,1,0:T(8,128)(2,1)S(1)}) custom-call(f32[256,1024]{1,0:T(8,128)S(1)} %fusion.sums_ref, f32[1,256,256]{2,1,0:T(8,128)S(1)} %copy-done, f32[1,64]{1,0:T(1,128)S(1)} %copy-done.3, bf16[8,2,2,64,1024]{4,3,2,1,0:T(8,128)(2,1)} %bitcast.12), custom_call_target="tpu_custom_call" | custom-call | tf_op jit(solution)/shard_map/pallas_call | solution.py:169
  88.2 0.0 copy-start.1
  88.2 29.2 %all_to_all.21.coded_ref = s32[16,72,128]{2,1,0:T(8,128)S(1)} all-to-all(s32[16,72,128]{2,1,0:T(8,128)S(1)} %get-tuple-element.15), channel_id=1, replica_groups=mesh['x'=4,'yl'=2,'core'=2,'z'=8,'yh'=2] {'z','yh'}, dimensions={0} | all-to-all | bytes 1179648 | tf_op jit(solution)/shard_map/all_to_all | solution.py:297
  117.4 0.0 copy-done.2
  117.4 2.2 %shard_map.75 = f32[16,8,128]{2,1,0:T(8,128)S(1)} custom-call(s32[1]{0:T(128)} %bitcast.3.worker_ref, s32[16,72,128]{2,1,0:T(8,128)S(1)} %all_to_all.21.coded_ref, bf16[8,2,2,64,1024]{4,3,2,1,0:T(8,128)(2,1)S(1)} %get-tuple-element.16.basis_ref, f32[1,256]{1,0:T(1,128)S(1)} %copy-done.2), custom_call_target="tpu_custom_call" | custom-call | tf_op jit(solution)/shard_map/pallas_call | solution.py:235
  119.6 12.9 %all_to_all.22.precond_ref = f32[16,8,128]{2,1,0:T(8,128)S(1)} all-to-all(f32[16,8,128]{2,1,0:T(8,128)S(1)} %shard_map.75), channel_id=1, replica_groups=mesh['x'=4,'yl'=2,'core'=2,'z'=8,'yh'=2] {'z','yh'}, dimensions={0} | all-to-all | bytes 131072 | tf_op jit(solution)/shard_map/all_to_all | solution.py:299
  132.5 0.5 shard_map.76
  133.0 10.7 %all_to_all.23.blocks_ref = f32[8,64,256]{2,1,0:T(8,128)S(1)} all-to-all(f32[8,64,256]{2,1,0:T(8,128)S(1)} %shard_map.76), channel_id=1, replica_groups=mesh['x'=4,'yl'=2,'core'=2,'z'=8,'yh'=2] {'x','yl'}, dimensions={0} | all-to-all | bytes 1048576 | tf_op jit(solution)/shard_map/all_to_all | solution.py:301
  143.7 4.1 %collective-permute-start.1 = (f32[8,64,256]{2,1,0:T(8,128)S(1)}, f32[8,64,256]{2,1,0:T(8,128)S(1)}, u32[]{:S(2)}, u32[]{:S(2)}) collective-permute-start(f32[8,64,256]{2,1,0:T(8,128)S(1)} %all_to_all.23.blocks_ref), channel_id=1, source_target_pairs={{0,16},{16,0},{1,17},{17,1},{2,18},{18,2},{3,19},{19,3},{4,20},{20... | collective-permute-start | bytes 1572872 | tf_op jit(solution)/shard_map/ppermute | solution.py:302
  147.8 1.4 shard_map.77.rest_0_
  149.2 0.1 collective-permute-done.1.blocks_ref
  149.4 1.4 shard_map.78
  (7 shorter events, 0.1 us)
Async XLA Ops:
  6.5 79.1 %all-gather.3.cloned.1.call-start = ((), (), s32[]{:S(2)}) async-start(), calls=%async_computation.4 | async-start | bytes 4718592 | tf_op jit(solution)/shard_map/all_gather | solution.py:288
  6.5 9.6 %collective-permute-start = (f32[64,1024]{1,0:T(8,128)}, f32[64,1024]{1,0:T(8,128)S(1)}, u32[]{:S(2)}, u32[]{:S(2)}) collective-permute-start(f32[64,1024]{1,0:T(8,128)} %bitcast.13), channel_id=1, source_target_pairs={{0,1},{1,0},{2,3},{3,2},{4,5},{5,4},{6,7},{7,6},{8,9},{9,8},{10,11... | collective-permute-start | bytes 786440 | tf_op jit(solution)/shard_map/ppermute | solution.py:277
  10.3 5.9 %copy-start.4 = (f32[1,64,1024]{2,1,0:T(8,128)S(1)}, f32[1,64,1024]{2,1,0:T(8,128)}, u32[]{:S(2)}) copy-start(f32[1,64,1024]{2,1,0:T(8,128)} %param.10) | copy-start | bytes 786436
  84.3 1.3 copy-start
  84.3 1.3 copy-start.3
  85.6 31.8 %copy-start.2 = (f32[1,256]{1,0:T(1,128)S(1)}, f32[1,256]{1,0:T(1,128)}, u32[]{:S(2)}) copy-start(f32[1,256]{1,0:T(1,128)} %small_ref.4) | copy-start | bytes 3076
  88.2 59.6 %copy-start.1 = (s32[16]{0:T(128)S(1)}, s32[16]{0:T(128)}, u32[]{:S(2)}) copy-start(s32[16]{0:T(128)} %owned_ref.5) | copy-start | bytes 196
  143.7 5.7 %collective-permute-start.1 = (f32[8,64,256]{2,1,0:T(8,128)S(1)}, f32[8,64,256]{2,1,0:T(8,128)S(1)}, u32[]{:S(2)}, u32[]{:S(2)}) collective-permute-start(f32[8,64,256]{2,1,0:T(8,128)S(1)} %all_to_all.23.blocks_ref), channel_id=1, source_target_pairs={{0,16},{16,0},{1,17},{17,1},{2,18},{18,2},{3,19},{19,3},{4,20},{20... | collective-permute-start | bytes 1572872 | tf_op jit(solution)/shard_map/ppermute | solution.py:302
Sparse Core Ops, SparseCore 0:
  17.3 58.7 all-gather.2

commit v6 on v5

--- a/solution.py
+++ b/solution.py
@@ -265,6 +265,11 @@
     )(precond, narrow_basis)
 
 
+def two_parts(value):
+    high = lax.reduce_precision(value, 8, 7)
+    return jnp.stack([high.astype(jnp.bfloat16), (value - high).astype(jnp.bfloat16)])
+
+
 def local(
     owned_layer, wide_side, narrow_side, wide_basis, narrow_basis, wide_values, narrow_values
 ):
@@ -276,12 +281,12 @@
 
     swapped = lax.ppermute(wide_basis[0], "yh", [(0, 1), (1, 0)])
     packed = pack_tokens(owned_layer, wide_side, narrow_side)
-    low = lax.axis_index("yh") == 0
-    held = jnp.stack(
-        [jnp.where(low, wide_basis[0], swapped), jnp.where(low, swapped, wide_basis[0])]
-    )
-    high = lax.reduce_precision(held, 8, 7)
-    held = jnp.stack([high.astype(jnp.bfloat16), (held - high).astype(jnp.bfloat16)], axis=1)
+    half = lax.axis_index("yh")
+    own = two_parts(wide_basis[0])
+    held = jnp.zeros((2,) + own.shape, own.dtype)
+    held = lax.dynamic_update_slice(held, own[None], (half, 0, 0, 0))
+    held = lax.optimization_barrier(held)
+    held = lax.dynamic_update_slice(held, two_parts(swapped)[None], (1 - half, 0, 0, 0))
     worker = lax.axis_index(WK).reshape(1)
     core = lax.axis_index("core").reshape(1)
     held, packed, worker, core = lax.optimization_barrier((held, packed, worker, core))

time: 158 us -> 158 us (level)
  no operation moved by 1% of the time
where the time goes in v6:
time: 158 us; the launch traced here: 157 us
  blocking collectives  119 us (75%)
  Pallas kernels  13.7 us (9%)
  between operations  13.6 us (9%)
  starting transfers between devices  7.86 us (5%)
    all_to_all x1, blocking collectives, local(): packed = lax.all_to_all(packed, GRP, 0, 0, tiled=True)  66.2 us
    all_to_all x1, blocking collectives, local(): coded = lax.all_to_all(coded, WK, 0, 0, tiled=True)  29.2 us
    all_to_all x1, blocking collectives, local(): precond = lax.all_to_all(precond, WK, 0, 0, tiled=True)  12.9 us
    all_to_all x1, blocking collectives, local(): spread = lax.all_to_all(spread, ('x', 'yl'), 0, 0, tiled=True)  10.7 us
    pallas_call x1, Pallas kernels, pack_tokens(): pl.pallas_call(pack_kernel, out_shape=jax.ShapeDtypeStruct(packed, wide_s...  5.73 us
    ppermute x1, starting transfers between devices, local(): other = lax.ppermute(spread, 'core', [(0, 1), (1, 0)])  4.11 us
    ppermute x1, starting transfers between devices, local(): swapped = lax.ppermute(wide_basis[0], 'yh', [(0, 1), (1, 0)])  3.74 us
  transfers between devices with their start and end apart: 3, of which 1 were waited for; matrix products, arithmetic and copies ran while one was open for 1% of the time, Pallas kernels for 5%

profile of v6, /device:TPU:1, one launch (start us, length us, event | category | flops | bytes accessed | tf_op | source)
XLA Modules:
  0.0 157.5 jit_solution(9569491448396359691)
XLA Ops:
  6.5 0.0 all-gather.3.cloned.1.call-start
  6.5 3.7 %collective-permute-start = (f32[64,1024]{1,0:T(8,128)}, f32[64,1024]{1,0:T(8,128)S(1)}, u32[]{:S(2)}, u32[]{:S(2)}) collective-permute-start(f32[64,1024]{1,0:T(8,128)} %bitcast.19), channel_id=1, source_target_pairs={{0,1},{1,0},{2,3},{3,2},{4,5},{5,4},{6,7},{7,6},{8,9},{9,8},{10,11... | collective-permute-start | bytes 786440 | tf_op jit(solution)/shard_map/ppermute | solution.py:282
  10.3 1.0 reduce-precision_convert_fusion.1
  11.3 0.1 broadcast_in_dim.9
  11.4 5.7 %shard_map.73 = bf16[16,128,1280]{2,1,0:T(8,128)(2,1)} custom-call(s32[16]{0:T(128)} %owned_ref.5, bf16[16,128,1024]{2,1,0:T(8,128)(2,1)} %wide_ref.1, bf16[16,128,256]{2,1,0:T(8,128)(2,1)} %narrow_ref.1), custom_call_target="tpu_custom_call" | custom-call | tf_op jit(solution)/shard_map/pallas_call | solution.py:56
  17.1 0.0 collective-permute-done
  17.2 0.0 copy-start.4
  17.2 0.8 copy-done.4
  18.0 0.0 all-gather.3.cloned.1.call-update
  18.0 66.2 %all_to_all.20 = bf16[16,128,1280]{2,1,0:T(8,128)(2,1)S(1)} all-to-all(bf16[16,128,1280]{2,1,0:T(8,128)(2,1)} %shard_map.73), channel_id=1, replica_groups=mesh['x'=4,'yl'=2,'core'=2,'z'=8,'yh'=2] {'x','yl','core'}, dimensions={0} | all-to-all | bytes 10485760 | tf_op jit(solution)/shard_map/all_to_all | solution.py:295
  84.2 1.3 fusion.sums_ref
  85.5 0.0 copy-start.2
  85.5 0.0 all-gather.3.cloned.1.call-done
  85.5 2.5 %shard_map.74 = (s32[16,72,128]{2,1,0:T(8,128)S(1)}, bf16[8,2,2,64,1024]{4,3,2,1,0:T(8,128)(2,1)S(1)}) custom-call(f32[256,1024]{1,0:T(8,128)S(1)} %fusion.sums_ref, f32[1,256,256]{2,1,0:T(8,128)S(1)} %copy-done, f32[1,64]{1,0:T(1,128)S(1)} %copy-done.3, bf16[8,2,2,64,1024]{4,3,2,1,0:T(8,128)(2,1)} %bitcast.18), custom_call_target="tpu_custom_call" | custom-call | tf_op jit(solution)/shard_map/pallas_call | solution.py:169
  88.1 0.0 copy-start.1
  88.1 29.2 %all_to_all.21.coded_ref = s32[16,72,128]{2,1,0:T(8,128)S(1)} all-to-all(s32[16,72,128]{2,1,0:T(8,128)S(1)} %get-tuple-element.15), channel_id=1, replica_groups=mesh['x'=4,'yl'=2,'core'=2,'z'=8,'yh'=2] {'z','yh'}, dimensions={0} | all-to-all | bytes 1179648 | tf_op jit(solution)/shard_map/all_to_all | solution.py:302
  117.3 2.2 %shard_map.75 = f32[16,8,128]{2,1,0:T(8,128)S(1)} custom-call(s32[1]{0:T(128)} %bitcast.5.worker_ref, s32[16,72,128]{2,1,0:T(8,128)S(1)} %all_to_all.21.coded_ref, bf16[8,2,2,64,1024]{4,3,2,1,0:T(8,128)(2,1)S(1)} %get-tuple-element.16.basis_ref, f32[1,256]{1,0:T(1,128)S(1)} %copy-done.2), custom_call_target="tpu_custom_call" | custom-call | tf_op jit(solution)/shard_map/pallas_call | solution.py:235
  119.5 12.9 %all_to_all.22.precond_ref = f32[16,8,128]{2,1,0:T(8,128)S(1)} all-to-all(f32[16,8,128]{2,1,0:T(8,128)S(1)} %shard_map.75), channel_id=1, replica_groups=mesh['x'=4,'yl'=2,'core'=2,'z'=8,'yh'=2] {'z','yh'}, dimensions={0} | all-to-all | bytes 131072 | tf_op jit(solution)/shard_map/all_to_all | solution.py:304
  132.4 0.5 shard_map.76
  132.9 10.7 %all_to_all.23.blocks_ref = f32[8,64,256]{2,1,0:T(8,128)S(1)} all-to-all(f32[8,64,256]{2,1,0:T(8,128)S(1)} %shard_map.76), channel_id=1, replica_groups=mesh['x'=4,'yl'=2,'core'=2,'z'=8,'yh'=2] {'x','yl'}, dimensions={0} | all-to-all | bytes 1048576 | tf_op jit(solution)/shard_map/all_to_all | solution.py:306
  143.6 4.1 %collective-permute-start.1 = (f32[8,64,256]{2,1,0:T(8,128)S(1)}, f32[8,64,256]{2,1,0:T(8,128)S(1)}, u32[]{:S(2)}, u32[]{:S(2)}) collective-permute-start(f32[8,64,256]{2,1,0:T(8,128)S(1)} %all_to_all.23.blocks_ref), channel_id=1, source_target_pairs={{0,16},{16,0},{1,17},{17,1},{2,18},{18,2},{3,19},{19,3},{4,20},{20... | collective-permute-start | bytes 1572872 | tf_op jit(solution)/shard_map/ppermute | solution.py:307
  147.7 1.4 shard_map.77.rest_0_
  149.1 0.1 collective-permute-done.1.blocks_ref
  149.2 1.4 shard_map.78
  (9 shorter events, 0.1 us)
Async XLA Ops:
  6.5 79.0 %all-gather.3.cloned.1.call-start = ((), (), s32[]{:S(2)}) async-start(), calls=%async_computation.4 | async-start | bytes 4718592 | tf_op jit(solution)/shard_map/all_gather | solution.py:293
  6.5 10.6 %collective-permute-start = (f32[64,1024]{1,0:T(8,128)}, f32[64,1024]{1,0:T(8,128)S(1)}, u32[]{:S(2)}, u32[]{:S(2)}) collective-permute-start(f32[64,1024]{1,0:T(8,128)} %bitcast.19), channel_id=1, source_target_pairs={{0,1},{1,0},{2,3},{3,2},{4,5},{5,4},{6,7},{7,6},{8,9},{9,8},{10,11... | collective-permute-start | bytes 786440 | tf_op jit(solution)/shard_map/ppermute | solution.py:282
  17.2 0.8 copy-start.4
  84.2 1.3 copy-start
  84.2 1.3 copy-start.3
  85.5 31.8 %copy-start.2 = (f32[1,256]{1,0:T(1,128)S(1)}, f32[1,256]{1,0:T(1,128)}, u32[]{:S(2)}) copy-start(f32[1,256]{1,0:T(1,128)} %small_ref.4) | copy-start | bytes 3076
  88.1 59.6 %copy-start.1 = (s32[16]{0:T(128)S(1)}, s32[16]{0:T(128)}, u32[]{:S(2)}) copy-start(s32[16]{0:T(128)} %owned_ref.5) | copy-start | bytes 196
  143.6 5.7 %collective-permute-start.1 = (f32[8,64,256]{2,1,0:T(8,128)S(1)}, f32[8,64,256]{2,1,0:T(8,128)S(1)}, u32[]{:S(2)}, u32[]{:S(2)}) collective-permute-start(f32[8,64,256]{2,1,0:T(8,128)S(1)} %all_to_all.23.blocks_ref), channel_id=1, source_target_pairs={{0,16},{16,0},{1,17},{17,1},{2,18},{18,2},{3,19},{19,3},{4,20},{20... | collective-permute-start | bytes 1572872 | tf_op jit(solution)/shard_map/ppermute | solution.py:307
Sparse Core Ops, SparseCore 0:
  18.2 57.7 all-gather.2

commit v7 on v5

--- a/solution.py
+++ b/solution.py
@@ -124,8 +124,12 @@
 
 def encode_kernel(sums_ref, small_ref, values_ref, held_ref, out_ref, basis_ref, sems):
     loads = [
-        pltpu.make_async_copy(held_ref.at[z], basis_ref.at[z], sems.at[z])
+        pltpu.make_async_copy(
+            held_ref.at[z, h, i], basis_ref.at[i, pl.ds((2 * z + h) * 64, 64)], sems.at[i, 2 * z + h]
+        )
+        for i in range(2)
         for z in range(held_ref.shape[0])
+        for h in range(2)
     ]
     for load in loads:
         load.start()
@@ -170,11 +174,11 @@
         encode_kernel,
         out_shape=(
             jax.ShapeDtypeStruct((workers, words, 128), jnp.int32),
-            jax.ShapeDtypeStruct(held.shape, held.dtype),
+            jax.ShapeDtypeStruct((2, wide, wide), held.dtype),
         ),
         in_specs=[pl.BlockSpec(memory_space=pltpu.VMEM)] * 3 + [pl.BlockSpec(memory_space=pl.ANY)],
         out_specs=(pl.BlockSpec(memory_space=pltpu.VMEM), pl.BlockSpec(memory_space=pltpu.VMEM)),
-        scratch_shapes=[pltpu.SemaphoreType.DMA((held.shape[0],))],
+        scratch_shapes=[pltpu.SemaphoreType.DMA((2, workers))],
         compiler_params=pltpu.CompilerParams(vmem_limit_bytes=ENCODE_GRANT),
     )(sums, narrow_basis, wide_values, held)
 
@@ -214,13 +218,7 @@
         worker_ref[0] * (2 * half) + lax.broadcasted_iota(jnp.int32, (2 * half, count), 0)
     )
     small = jnp.sum(jnp.where(own, small_ref[...], 0.0), axis=1, keepdims=True)
-    high, low = (
-        jnp.concatenate(
-            [basis_ref[z, h, i] for z in range(basis_ref.shape[0]) for h in range(basis_ref.shape[1])],
-            axis=0,
-        )
-        for i in range(2)
-    )
+    high, low = basis_ref[0], basis_ref[1]
     rotated = product(gradient, high, low, 0)
     scaled = rotated / (small * wide_values + DAMPING)
     precond = product(scaled, high, low, 1)

time: 158 us -> 158 us (level)
  no operation moved by 1% of the time
where the time goes in v7:
time: 158 us
  blocking collectives  120 us (76%)
  Pallas kernels  14.3 us (9%)
  between operations  13.5 us (9%)
  starting transfers between devices  7.86 us (5%)
    all_to_all x1, blocking collectives, local(): packed = lax.all_to_all(packed, GRP, 0, 0, tiled=True)  67.2 us
    all_to_all x1, blocking collectives, local(): coded = lax.all_to_all(coded, WK, 0, 0, tiled=True)  29.2 us
    all_to_all x1, blocking collectives, local(): precond = lax.all_to_all(precond, WK, 0, 0, tiled=True)  12.9 us
    all_to_all x1, blocking collectives, local(): spread = lax.all_to_all(spread, ('x', 'yl'), 0, 0, tiled=True)  10.7 us
    pallas_call x1, Pallas kernels, pack_tokens(): pl.pallas_call(pack_kernel, out_shape=jax.ShapeDtypeStruct(packed, wide_s...  5.86 us
    ppermute x1, starting transfers between devices, local(): other = lax.ppermute(spread, 'core', [(0, 1), (1, 0)])  4.11 us
    ppermute x1, starting transfers between devices, local(): swapped = lax.ppermute(wide_basis[0], 'yh', [(0, 1), (1, 0)])  3.74 us
  transfers between devices with their start and end apart: 3, of which 1 were waited for; matrix products, arithmetic and copies ran while one was open for 1% of the time, Pallas kernels for 5%

profile of v7, /device:TPU:1, one launch (start us, length us, event | category | flops | bytes accessed | tf_op | source)
XLA Modules:
  0.0 158.1 jit_solution(12422718843289775913)
XLA Ops:
  6.5 0.0 all-gather.3.cloned.1.call-start
  6.5 3.7 %collective-permute-start = (f32[64,1024]{1,0:T(8,128)}, f32[64,1024]{1,0:T(8,128)S(1)}, u32[]{:S(2)}, u32[]{:S(2)}) collective-permute-start(f32[64,1024]{1,0:T(8,128)} %bitcast.13), channel_id=1, source_target_pairs={{0,1},{1,0},{2,3},{3,2},{4,5},{5,4},{6,7},{7,6},{8,9},{9,8},{10,11... | collective-permute-start | bytes 786440 | tf_op jit(solution)/shard_map/ppermute | solution.py:275
  10.3 5.9 %shard_map.73 = bf16[16,128,1280]{2,1,0:T(8,128)(2,1)} custom-call(s32[16]{0:T(128)} %owned_ref.5, bf16[16,128,1024]{2,1,0:T(8,128)(2,1)} %wide_ref.1, bf16[16,128,256]{2,1,0:T(8,128)(2,1)} %narrow_ref.1), custom_call_target="tpu_custom_call" | custom-call | tf_op jit(solution)/shard_map/pallas_call | solution.py:56
  16.1 0.0 collective-permute-done
  16.2 0.0 copy-done.4
  16.2 0.1 reduce-precision_convert_fusion
  16.3 0.8 pad_maximum_fusion.1
  17.1 0.0 all-gather.3.cloned.1.call-update
  17.2 67.2 %all_to_all.20 = bf16[16,128,1280]{2,1,0:T(8,128)(2,1)S(1)} all-to-all(bf16[16,128,1280]{2,1,0:T(8,128)(2,1)} %shard_map.73), channel_id=1, replica_groups=mesh['x'=4,'yl'=2,'core'=2,'z'=8,'yh'=2] {'x','yl','core'}, dimensions={0} | all-to-all | bytes 10485760 | tf_op jit(solution)/shard_map/all_to_all | solution.py:288
  84.3 1.3 fusion.sums_ref
  85.6 0.0 copy-start.2
  85.6 0.0 all-gather.3.cloned.1.call-done
  85.6 0.0 copy-done
  85.7 3.1 %shard_map.74 = (s32[16,72,128]{2,1,0:T(8,128)S(1)}, bf16[2,1024,1024]{2,1,0:T(8,128)(2,1)S(1)}) custom-call(f32[256,1024]{1,0:T(8,128)S(1)} %fusion.sums_ref, f32[1,256,256]{2,1,0:T(8,128)S(1)} %copy-done, f32[1,64]{1,0:T(1,128)S(1)} %copy-done.3, bf16[8,2,2,64,1024]{4,3,2,1,0:T(8,128)(2,1)} %bitcast.12), custom_call_target="tpu_custom_call" | custom-call | tf_op jit(solution)/shard_map/pallas_call | solution.py:173
  88.7 0.0 copy-start.1
  88.7 29.2 %all_to_all.21.coded_ref = s32[16,72,128]{2,1,0:T(8,128)S(1)} all-to-all(s32[16,72,128]{2,1,0:T(8,128)S(1)} %get-tuple-element.15), channel_id=1, replica_groups=mesh['x'=4,'yl'=2,'core'=2,'z'=8,'yh'=2] {'z','yh'}, dimensions={0} | all-to-all | bytes 1179648 | tf_op jit(solution)/shard_map/all_to_all | solution.py:295
  117.9 2.2 %shard_map.75 = f32[16,8,128]{2,1,0:T(8,128)S(1)} custom-call(s32[1]{0:T(128)} %bitcast.3.worker_ref, s32[16,72,128]{2,1,0:T(8,128)S(1)} %all_to_all.21.coded_ref, bf16[2,1024,1024]{2,1,0:T(8,128)(2,1)S(1)} %get-tuple-element.16.basis_ref, f32[1,256]{1,0:T(1,128)S(1)} %copy-done.2), custom_call_target="tpu_custom_call" | custom-call | tf_op jit(solution)/shard_map/pallas_call | solution.py:233
  120.1 12.9 %all_to_all.22.precond_ref = f32[16,8,128]{2,1,0:T(8,128)S(1)} all-to-all(f32[16,8,128]{2,1,0:T(8,128)S(1)} %shard_map.75), channel_id=1, replica_groups=mesh['x'=4,'yl'=2,'core'=2,'z'=8,'yh'=2] {'z','yh'}, dimensions={0} | all-to-all | bytes 131072 | tf_op jit(solution)/shard_map/all_to_all | solution.py:297
  133.0 0.5 shard_map.76
  133.5 10.7 %all_to_all.23.blocks_ref = f32[8,64,256]{2,1,0:T(8,128)S(1)} all-to-all(f32[8,64,256]{2,1,0:T(8,128)S(1)} %shard_map.76), channel_id=1, replica_groups=mesh['x'=4,'yl'=2,'core'=2,'z'=8,'yh'=2] {'x','yl'}, dimensions={0} | all-to-all | bytes 1048576 | tf_op jit(solution)/shard_map/all_to_all | solution.py:299
  144.2 4.1 %collective-permute-start.1 = (f32[8,64,256]{2,1,0:T(8,128)S(1)}, f32[8,64,256]{2,1,0:T(8,128)S(1)}, u32[]{:S(2)}, u32[]{:S(2)}) collective-permute-start(f32[8,64,256]{2,1,0:T(8,128)S(1)} %all_to_all.23.blocks_ref), channel_id=1, source_target_pairs={{0,16},{16,0},{1,17},{17,1},{2,18},{18,2},{3,19},{19,3},{4,20},{20... | collective-permute-start | bytes 1572872 | tf_op jit(solution)/shard_map/ppermute | solution.py:300
  148.3 1.4 shard_map.77.rest_0_
  149.7 0.1 collective-permute-done.1.blocks_ref
  149.9 1.4 shard_map.78
  (7 shorter events, 0.1 us)
Async XLA Ops:
  6.5 79.1 %all-gather.3.cloned.1.call-start = ((), (), s32[]{:S(2)}) async-start(), calls=%async_computation.4 | async-start | bytes 4718592 | tf_op jit(solution)/shard_map/all_gather | solution.py:286
  6.5 9.6 %collective-permute-start = (f32[64,1024]{1,0:T(8,128)}, f32[64,1024]{1,0:T(8,128)S(1)}, u32[]{:S(2)}, u32[]{:S(2)}) collective-permute-start(f32[64,1024]{1,0:T(8,128)} %bitcast.13), channel_id=1, source_target_pairs={{0,1},{1,0},{2,3},{3,2},{4,5},{5,4},{6,7},{7,6},{8,9},{9,8},{10,11... | collective-permute-start | bytes 786440 | tf_op jit(solution)/shard_map/ppermute | solution.py:275
  10.3 5.9 %copy-start.4 = (f32[1,64,1024]{2,1,0:T(8,128)S(1)}, f32[1,64,1024]{2,1,0:T(8,128)}, u32[]{:S(2)}) copy-start(f32[1,64,1024]{2,1,0:T(8,128)} %param.10) | copy-start | bytes 786436
  84.3 1.3 copy-start
  84.3 1.3 copy-start.3
  85.6 32.3 %copy-start.2 = (f32[1,256]{1,0:T(1,128)S(1)}, f32[1,256]{1,0:T(1,128)}, u32[]{:S(2)}) copy-start(f32[1,256]{1,0:T(1,128)} %small_ref.4) | copy-start | bytes 3076
  88.7 59.6 %copy-start.1 = (s32[16]{0:T(128)S(1)}, s32[16]{0:T(128)}, u32[]{:S(2)}) copy-start(s32[16]{0:T(128)} %owned_ref.5) | copy-start | bytes 196
  144.2 5.7 %collective-permute-start.1 = (f32[8,64,256]{2,1,0:T(8,128)S(1)}, f32[8,64,256]{2,1,0:T(8,128)S(1)}, u32[]{:S(2)}, u32[]{:S(2)}) collective-permute-start(f32[8,64,256]{2,1,0:T(8,128)S(1)} %all_to_all.23.blocks_ref), channel_id=1, source_target_pairs={{0,16},{16,0},{1,17},{17,1},{2,18},{18,2},{3,19},{19,3},{4,20},{20... | collective-permute-start | bytes 1572872 | tf_op jit(solution)/shard_map/ppermute | solution.py:300
Sparse Core Ops, SparseCore 0:
  17.3 58.7 all-gather.2
